TPU v7x, 128 devices: a whole 4x4x4 slice. The times are simulated.
128 devices in a mesh: seq: 64 (over z, x, y), tensor: 2 (over core).
Axes of the slice: x: 4, y: 4, z: 4, core: 2. Of those that a mesh axis runs over, the one named last changes fastest.
Arguments:
- tokens: bfloat16 [8192, 1536], P('seq'), may hold values from -6 to 6
- cotangent: bfloat16 [8192, 1536], P('seq'), may hold values from -6 to 6
- lengths: int32 [8], replicated, may hold values from 200 to 4096, as said below
- norm1_gain: float32 [1536], replicated, may hold values from 0.5 to 1.5
- w_query: bfloat16 [1536, 12, 128], P(None, 'tensor'), may hold values from -0.15625 to 0.15625
- b_query: bfloat16 [12, 128], P('tensor'), may hold values from -3 to 3
- w_key: bfloat16 [1536, 2, 128], P(None, 'tensor'), may hold values from -0.15625 to 0.15625
- b_key: bfloat16 [2, 128], P('tensor'), may hold values from -3 to 3
- w_value: bfloat16 [1536, 2, 128], P(None, 'tensor'), may hold values from -0.15625 to 0.15625
- b_value: bfloat16 [2, 128], P('tensor'), may hold values from -3 to 3
- w_out: bfloat16 [12, 128, 1536], P('tensor'), may hold values from -1.25 to 1.25
- norm2_gain: float32 [1536], replicated, may hold values from 0.5 to 1.5
- w_gate: bfloat16 [1536, 8960], P(None, 'tensor'), may hold values from -0.15625 to 0.15625
- w_up: bfloat16 [1536, 8960], P(None, 'tensor'), may hold values from -0.15625 to 0.15625
- w_down: bfloat16 [8960, 1536], P('tensor'), may hold values from -0.25 to 0.25
Outputs:
- output: float32 [8192, 1536], P('seq')
- grad_tokens: float32 [8192, 1536], P('seq')
- grad_norm1: float32 [1536], P('seq')
- grad_w_query: float32 [1536, 12, 128], P('seq', 'tensor')
- grad_b_query: float32 [12, 128], P('tensor', 'seq')
- grad_w_key: float32 [1536, 2, 128], P('seq', 'tensor')
- grad_b_key: float32 [2, 128], P('tensor', 'seq')
- grad_w_value: float32 [1536, 2, 128], P('seq', 'tensor')
- grad_b_value: float32 [2, 128], P('tensor', 'seq')
- grad_w_out: float32 [12, 128, 1536], P('tensor', None, 'seq')
- grad_norm2: float32 [1536], P('seq')
- grad_w_gate: float32 [1536, 8960], P('seq', 'tensor')
- grad_w_up: float32 [1536, 8960], P('seq', 'tensor')
- grad_w_down: float32 [8960, 1536], P('tensor', 'seq')
Inputs may be any that keep to these rules, and one draw needn't show every extreme that they name: The 8 lengths sum to 8192; each is at least 200; exactly one, at a place in the pack drawn from the seed, is 4096 long, and all others are shorter.
All inputs are finite; a program needn't handle non-finite values.
Results may differ from a plain program's by a relative error of at most 0.035.
Values may be sent and summed in bfloat16 or wider, within the bound.
A program may use at most 320 MiB of HBM per device.

v0:
```python
import math

import jax
import jax.numpy as jnp
from jax import lax
from jax.experimental import pallas as pl
from jax.experimental.pallas import tpu as pltpu
from jax.sharding import PartitionSpec as P

MESH = pl.DeviceIdType.MESH
F32 = jnp.float32
BF16 = jnp.bfloat16
VMEM_BYTES = 60 * 1024 * 1024
AXES = ("z", "x", "y")
STRIDE = {"z": 16, "x": 4, "y": 1}


def coords():
    s = lax.axis_index("seq")
    return {"z": s // 16, "x": (s // 4) % 4, "y": s % 4}


def peer(axis, k):
    s = lax.axis_index("seq")
    c = coords()[axis]
    return (s + STRIDE[axis] * ((c + k) % 4 - c), lax.axis_index("tensor"))


def partner():
    return (lax.axis_index("seq"), 1 - lax.axis_index("tensor"))


def barrier(axes=AXES, core=False):
    bar = pltpu.get_barrier_semaphore()
    ids = [peer(a, k) for a in axes for k in (1, 2, 3)]
    if core:
        ids.append(partner())
    for d in ids:
        pl.semaphore_signal(bar, inc=1, device_id=d, device_id_type=MESH)
    pl.semaphore_wait(bar, len(ids))


def remote(src, dst, send, recv, device):
    return pltpu.make_async_remote_copy(
        src_ref=src, dst_ref=dst, send_sem=send, recv_sem=recv, device_id=device, device_id_type=MESH
    )


DMA = pltpu.SemaphoreType.DMA


KV_CHUNK = (
    (0, 48, ("z", "x", "y")),
    (48, 48, ("x", "y", "z")),
    (96, 32, ("y", "z", "x")),
)


def kv_rows(kb, v):
    return pl.ds(pl.multiple_of((kb // 4) * 128 + v * 64 + (kb % 4) * Q_BLK, Q_BLK), Q_BLK)


def kv_index(done, c, r0, rn):
    return tuple(slice(None) if a in done else c[a] for a in AXES) + (pl.ds(r0, rn), slice(None))


def rope_tables(len_ref):
    lane = lax.broadcasted_iota(jnp.int32, (128, 128), 1)
    pos = lax.broadcasted_iota(jnp.int32, (128, 128), 0) * 64 + lax.axis_index("seq")
    rel = (pos - doc_bounds(pos, len_ref)).astype(F32)
    inv_freq = jnp.exp(-(2.0 * (lane % 64).astype(F32) / 128) * math.log(10000.0))
    angle = rel * inv_freq
    sin = jnp.sin(angle)
    return jnp.cos(angle), jnp.where(lane < 64, -sin, sin)


def swap_halves(v):
    return pltpu.roll(v, 64, 1)


def qkv_gather(tokens, gain, wq, wk, wv, bq, bk, bv, lengths):
    def body(len_ref, t_ref, g_ref, wq_ref, wk_ref, wv_ref, bq_ref, bk_ref, bv_ref,
             q_out, out, nt_out, cos_out, sin_out, wq_buf, loc, send, recv):
        c = coords()
        load = pltpu.make_async_copy(wq_ref, wq_buf, loc)
        load.start()
        x = t_ref[...].astype(F32)
        inv = lax.rsqrt(jnp.mean(x * x, axis=1, keepdims=True) + 1e-06)
        normed = (x * inv * g_ref[0:1, :]).astype(BF16)
        cos, sin = rope_tables(len_ref)
        cos_out[...], sin_out[...] = cos, sin
        k_pre = jnp.dot(normed, wk_ref[...], preferred_element_type=F32) + bk_ref[...].astype(F32)
        v_pre = jnp.dot(normed, wv_ref[...], preferred_element_type=F32) + bv_ref[...].astype(F32)
        k_rot = (k_pre * cos + swap_halves(k_pre) * sin).astype(BF16)
        v_low = v_pre.astype(BF16)
        out[c["z"], c["x"], c["y"]] = jnp.concatenate([k_rot[:64], v_low[:64], k_rot[64:], v_low[64:]], axis=0)
        barrier()
        parts = [(r0 + 128 * chunk, rn, order) for chunk in range(2) for r0, rn, order in KV_CHUNK]
        pending = [[] for _ in parts]

        def send_stage(stage):
            for p, (r0, rn, order) in enumerate(parts):
                for copy in pending[p]:
                    copy.wait()
                pending[p] = []
                idx = kv_index(order[:stage], c, r0, rn)
                for k in (1, 2, 3):
                    n = (p * 3 + stage) * 3 + k - 1
                    copy = remote(out.at[idx], out.at[idx], send.at[n], recv.at[n], peer(order[stage], k))
                    copy.start()
                    pending[p].append(copy)

        send_stage(0)
        load.wait()
        for h in range(6):
            q = jnp.dot(normed, wq_buf[h], preferred_element_type=F32) + bq_ref[h : h + 1, :].astype(F32)
            q = (q * cos + swap_halves(q) * sin).astype(BF16)
            q_out[:, h * Q_BLK : (h + 1) * Q_BLK, :] = q.reshape(8, Q_BLK, 128)
        send_stage(1)
        nt_out[...] = normed.T
        send_stage(2)
        for copies in pending:
            for copy in copies:
                copy.wait()

    vm, sm = pl.BlockSpec(memory_space=pltpu.VMEM), pl.BlockSpec(memory_space=pltpu.SMEM)
    return pl.pallas_call(
        body,
        out_shape=(
            jax.ShapeDtypeStruct((8, 96, 128), BF16),
            jax.ShapeDtypeStruct((4, 4, 4, 256, 128), BF16),
            jax.ShapeDtypeStruct((1536, 128), BF16),
            jax.ShapeDtypeStruct((128, 128), F32),
            jax.ShapeDtypeStruct((128, 128), F32),
        ),
        in_specs=[sm, vm, vm, pl.BlockSpec(memory_space=pl.ANY)] + [vm] * 5,
        out_specs=(vm,) * 5,
        scratch_shapes=[pltpu.VMEM((6, 1536, 128), BF16), DMA, DMA((54,)), DMA((54,))],
        compiler_params=pltpu.CompilerParams(collective_id=0, has_side_effects=True, vmem_limit_bytes=VMEM_BYTES),
        name="qkv_gather",
    )(lengths, tokens, gain, wq, wk, wv, bq, bk, bv)


Q_BLK = 16
BLK = Q_BLK * 64
SCALE = 1.0 / math.sqrt(128)
SCALE2 = SCALE / math.log(2.0)


def doc_bounds(pos, len_ref):
    start = jnp.zeros_like(pos)
    end = jnp.int32(0)
    for j in range(8):
        end = end + len_ref[j]
        start = jnp.where(pos >= end, end, start)
    return start


def doc_start_scalar(pos, len_ref):
    start, end = jnp.int32(0), jnp.int32(0)
    for j in range(8):
        end = end + len_ref[j]
        start = jnp.where(pos >= end, end, start)
    return start


def attn_forward(q, kv, w_out, lengths):
    def body(len_ref, q_ref, kv_hbm, wo_hbm, part_ref, out_ref, low_ref, lse_ref, kv_ref, wo_ref, loc):
        loads = [
            pltpu.make_async_copy(kv_hbm.at[:, pl.ds(0, 128), :], kv_ref.at[:, pl.ds(0, 128), :], loc.at[0]),
            pltpu.make_async_copy(kv_hbm.at[:, pl.ds(128, 128), :], kv_ref.at[:, pl.ds(128, 128), :], loc.at[1]),
            pltpu.make_async_copy(wo_hbm, wo_ref, loc.at[2]),
        ]
        for copy in loads:
            copy.start()
        dev = lax.axis_index("seq")
        col = lax.broadcasted_iota(jnp.int32, (96, BLK), 1)
        key_off = (col % Q_BLK) * 64 + col // Q_BLK
        row_off = (lax.broadcasted_iota(jnp.int32, (96, 1), 0) % Q_BLK) * 64 + dev

        def q_step(qb, _):
            q_blk = q_ref[qb]
            pos_q = row_off + qb * BLK
            start_q = doc_bounds(pos_q, len_ref)
            lo = doc_start_scalar(qb * BLK + dev, len_ref) // BLK

            def k_step(kb, carry):
                m, l, acc = carry
                k_blk = kv_ref[:, kv_rows(kb, 0), :].reshape(BLK, 128)
                v_blk = kv_ref[:, kv_rows(kb, 1), :].reshape(BLK, 128)
                s = lax.dot_general(q_blk, k_blk, (((1,), (1,)), ((), ())), preferred_element_type=F32)
                pos_k = key_off + kb * BLK
                vis = (pos_k <= pos_q) & (pos_k >= start_q)
                s = jnp.where(vis, s * SCALE2, -1e30)
                m_new = jnp.maximum(m, jnp.max(s, axis=1, keepdims=True))
                p = jnp.where(vis, jnp.exp2(s - m_new), 0.0)
                a = jnp.exp2(m - m_new)
                l = l * a + jnp.sum(p, axis=1, keepdims=True)
                acc = acc * a + jnp.dot(p.astype(BF16), v_blk, preferred_element_type=F32)
                return m_new, l, acc

            init = (jnp.full((96, 1), -1e30, F32), jnp.zeros((96, 1), F32), jnp.zeros((96, 128), F32))
            m, l, acc = lax.fori_loop(lo, qb + 1, k_step, init)
            attn = acc / l
            out_ref[qb] = attn
            low = attn.astype(BF16)
            for h in range(6):
                rows = pl.ds(pl.multiple_of(qb * Q_BLK, Q_BLK), Q_BLK)
                low_ref[rows, h * 128 : (h + 1) * 128] = low[h * Q_BLK : (h + 1) * Q_BLK]
            lse_ref[qb] = jnp.broadcast_to(m + jnp.log2(l), (96, 128)).T[0:1]
            return 0

        loads[0].wait()
        lax.fori_loop(0, 4, q_step, 0)
        loads[1].wait()
        lax.fori_loop(4, 8, q_step, 0)
        loads[2].wait()
        part_ref[...] = jnp.dot(low_ref[...], wo_ref[...], preferred_element_type=F32)

    vm = pl.BlockSpec(memory_space=pltpu.VMEM)
    return pl.pallas_call(
        body,
        out_shape=(
            jax.ShapeDtypeStruct((128, 1536), F32),
            jax.ShapeDtypeStruct((8, 96, 128), F32),
            jax.ShapeDtypeStruct((128, 768), BF16),
            jax.ShapeDtypeStruct((8, 1, 96), F32),
        ),
        in_specs=[pl.BlockSpec(memory_space=pltpu.SMEM), vm] + [pl.BlockSpec(memory_space=pl.ANY)] * 2,
        out_specs=(vm,) * 4,
        scratch_shapes=[pltpu.VMEM((64, 256, 128), BF16), pltpu.VMEM((768, 1536), BF16), DMA((3,))],
        compiler_params=pltpu.CompilerParams(vmem_limit_bytes=VMEM_BYTES),
        name="attn_forward",
    )(lengths, q, kv, w_out)


FC = 1152


def nt(a, b):
    return lax.dot_general(a, b, (((1,), (1,)), ((), ())), preferred_element_type=F32)


def mm(a, b):
    return jnp.dot(a, b, preferred_element_type=F32)


def col_start(c):
    return pl.multiple_of(jnp.minimum(c * FC, 4480 - FC), 128)


MLP_AXES = (("z", "x", "y"), ("x", "y", "z"), ("y", "z", "x"))


def feed_forward(branch, attn, tokens, cot, gain, w_out, w_gate, w_up, w_down):
    def body(br_ref, at_ref, t_ref, c_ref, g_ref, wo_hbm, wg_hbm, wu_hbm, wd_hbm,
             out_ref, gmid_ref, bt_ref, ga_ref, delta_ref, dn_ref, x0, x1, x2, g0, g1, g2,
             wo_ref, wg, wu, wd, got_br, acc, got, mid_ref, norm_ref, nt_ref, ct_ref, act, w_sem, loc, send, recv):
        xs, gs = (x0, x1, x2), (g0, g1, g2)
        c = coords()
        turn = c["z"] + c["x"] + c["y"]
        sems = iter(range(64))

        def load(j):
            cols = pl.ds(col_start((turn + j) % 4), FC)
            b = j % 2
            copies = [
                pltpu.make_async_copy(wg_hbm.at[:, cols], wg.at[b], w_sem.at[b, 0]),
                pltpu.make_async_copy(wu_hbm.at[:, cols], wu.at[b], w_sem.at[b, 1]),
                pltpu.make_async_copy(wd_hbm.at[cols, :], wd.at[b], w_sem.at[b, 2]),
            ]
            for copy in copies:
                copy.start()
            return copies

        loads = [load(0), load(1)]
        barrier(core=True)

        def push(src, dst, device):
            n = next(sems)
            copy = remote(src, dst, send.at[n], recv.at[n], device)
            copy.start()
            return copy

        later = []
        ex = push(br_ref, got_br, partner())
        ct_ref[...] = c_ref[...].T
        own = [pltpu.make_async_copy(ct_ref, x2.at[:, pl.ds(0, 128)], loc.at[3])]
        own[0].start()
        for k in (1, 2, 3):
            later.append(push(ct_ref, x2.at[:, pl.ds(k * 128, 128)], peer("y", k)))
        ex.wait()
        mid = t_ref[...].astype(F32) + (br_ref[...] + got_br[...])
        mid_ref[...] = mid
        inv = lax.rsqrt(jnp.mean(mid * mid, axis=1, keepdims=True) + 1e-06)
        normed = (mid * inv * g_ref[1:2, :]).astype(BF16)
        norm_ref[...] = normed
        nt_ref[...] = normed.T
        own.append(pltpu.make_async_copy(nt_ref, x0.at[:, pl.ds(0, 128)], loc.at[4]))
        own.append(pltpu.make_async_copy(nt_ref, x1.at[:, pl.ds(0, 128)], loc.at[5]))
        own.append(pltpu.make_async_copy(wo_hbm, wo_ref, loc.at[6]))
        for copy in own[1:]:
            copy.start()
        for k in (1, 2, 3):
            for m, w in ((0, "z"), (1, "x")):
                later.append(push(nt_ref, xs[m].at[:, pl.ds(k * 128, 128)], peer(w, k)))

        lane = lax.broadcasted_iota(jnp.int32, (128, FC), 1)
        for j in range(4):
            b = j % 2
            d = (turn + j) % 4
            for copy in loads[j]:
                copy.wait()
            n = norm_ref[...]
            gate = mm(n, wg[b])
            up = mm(n, wu[b])
            gh = nt(c_ref[...], wd[b])
            sig = 1.0 / (1.0 + jnp.exp(-gate))
            silu = gate * sig
            hidden = (silu * up).astype(BF16)
            g_gate = (gh * up * sig * (1.0 + gate * (1.0 - sig))).astype(BF16)
            g_up = (gh * silu).astype(BF16)
            vals = (g_gate, g_up, hidden)
            for m in range(3):
                act[m, j] = vals[m]
            twice = (lane < 128) & (d == 3)
            zero = jnp.zeros((128, FC), BF16)
            hidden, g_gate, g_up = (jnp.where(twice, zero, v) for v in (hidden, g_gate, g_up))
            add_o = mm(hidden, wd[b])
            add_g = nt(g_gate, wg[b]) + nt(g_up, wu[b])
            if j == 0:
                acc[0], acc[1] = add_o, add_g
            else:
                acc[0] += add_o
                acc[1] += add_g
            if j + 2 < 4:
                loads.append(load(j + 2))
            for m in range(3):
                w = MLP_AXES[m][0]
                k = (d + 4 - c[w]) % 4
                slot = pl.ds(pl.multiple_of(k * 128, 128), 128)

                @pl.when(k == 0)
                def _():
                    pltpu.make_async_copy(act.at[m, j], gs[m].at[pl.ds(0, 128), :], loc.at[m]).start()

                @pl.when(k != 0)
                def _():
                    remote(
                        act.at[m, j], gs[m].at[slot, :], send.at[32 + m * 4 + j], recv.at[32 + m * 4 + k], peer(w, k)
                    ).start()

        dn_ref[...] = jnp.sum(acc[1] * mid_ref[...] * inv, axis=0, keepdims=True)
        ex = [push(acc.at[1], got.at[1], partner()), push(acc.at[0], got.at[0], partner())]
        cot_f = c_ref[...].astype(F32)
        ex[0].wait()
        gn = acc[1] + got[1]
        mid = mid_ref[...]
        scaled = gn * g_ref[1:2, :]
        g_mid = cot_f + (inv * scaled - mid * (inv * inv * inv) * jnp.mean(scaled * mid, axis=1, keepdims=True))
        gmid_ref[...] = g_mid
        own[3].wait()
        branch_low = g_mid.astype(BF16)
        bt_ref[...] = branch_low.T
        g_attn = nt(branch_low, wo_ref[...]).astype(BF16)
        for h in range(6):
            ga_ref[:, h * Q_BLK : (h + 1) * Q_BLK, :] = g_attn[:, h * 128 : (h + 1) * 128].reshape(8, Q_BLK, 128)
        for qb in range(8):
            delta_ref[qb] = jnp.sum((ga_ref[qb].astype(F32) * at_ref[qb]).T, axis=0, keepdims=True)
        ex[1].wait()
        out_ref[...] = mid_ref[...] + (acc[0] + got[0])
        for copy in later + own[:3]:
            copy.wait()
        for m in range(3):
            w = MLP_AXES[m][0]
            pltpu.make_async_copy(act.at[m, 0], gs[m].at[pl.ds(0, 128), :], loc.at[m]).wait()
            for j in range(4):
                k = ((turn + j) % 4 + 4 - c[w]) % 4

                @pl.when(k != 0)
                def _():
                    slot = pl.ds(pl.multiple_of(k * 128, 128), 128)
                    remote(
                        act.at[m, j], gs[m].at[slot, :], send.at[32 + m * 4 + j], recv.at[32 + m * 4 + k], peer(w, k)
                    ).wait()

    f32 = lambda *s: jax.ShapeDtypeStruct(s, F32)
    b16 = lambda *s: jax.ShapeDtypeStruct(s, BF16)
    vm, hbm = pl.BlockSpec(memory_space=pltpu.VMEM), pl.BlockSpec(memory_space=pl.ANY)
    return pl.pallas_call(
        body,
        out_shape=(f32(128, 1536), f32(128, 1536), b16(1536, 128), b16(8, 96, 128), f32(8, 1, 96), f32(1, 1536))
        + (b16(1536, 512),) * 3
        + (b16(512, FC),) * 3,
        in_specs=[vm] * 5 + [hbm] * 4,
        out_specs=(vm,) * 6 + (hbm,) * 6,
        scratch_shapes=[
            pltpu.VMEM((768, 1536), BF16),
            pltpu.VMEM((2, 1536, FC), BF16),
            pltpu.VMEM((2, 1536, FC), BF16),
            pltpu.VMEM((2, FC, 1536), BF16),
            pltpu.VMEM((128, 1536), F32),
            pltpu.VMEM((2, 128, 1536), F32),
            pltpu.VMEM((2, 128, 1536), F32),
            pltpu.VMEM((128, 1536), F32),
            pltpu.VMEM((128, 1536), BF16),
            pltpu.VMEM((1536, 128), BF16),
            pltpu.VMEM((1536, 128), BF16),
            pltpu.VMEM((3, 4, 128, FC), BF16),
            DMA((2, 3)),
            DMA((7,)),
            DMA((64,)),
            DMA((64,)),
        ],
        compiler_params=pltpu.CompilerParams(collective_id=4, has_side_effects=True, vmem_limit_bytes=VMEM_BYTES),
        name="feed_forward",
    )(branch, attn, tokens, cot, gain, w_out, w_gate, w_up, w_down)


OUT_ORDERS = (("z", "x", "y"), ("x", "y", "z"), ("y", "z", "x"))
QKV_PARTS = ((0, 384, ("z", "x", "y")), (384, 768, ("x", "y", "z")), (768, 1024, ("y", "z", "x")))


def slab_products(buf, left, rhs, order):
    def blocks(v, places):
        return jnp.concatenate([v[o * 24 : (o + 1) * 24] for o in places], axis=0)

    if order[0] == "z":
        for z in range(4):
            buf[z] = mm(left[z * 384 : (z + 1) * 384, :], rhs).astype(BF16)
    elif order[0] == "x":
        for x in range(4):
            lhs = jnp.concatenate([left[z * 384 + x * 96 : z * 384 + (x + 1) * 96, :] for z in range(4)], axis=0)
            buf[x] = blocks(mm(lhs, rhs), [z * 4 + y for y in range(4) for z in range(4)]).astype(BF16)
    else:
        for z in range(4):
            v = blocks(mm(left[z * 384 : (z + 1) * 384, :], rhs), [x * 4 + y for y in range(4) for x in range(4)])
            v = v.astype(BF16)
            for y in range(4):
                buf[y, z * 96 : (z + 1) * 96] = v[y * 96 : (y + 1) * 96]


def sum_first(buf, got, copies, own):
    for copy in copies:
        copy.wait()
    total = buf[own].astype(F32)
    for k in range(3):
        total = total + got[k].astype(F32)
    buf[own] = total.astype(BF16)


def backward(xs_in, gs_in, q, g, kv, lse, delta, branch_t, attn_low, lengths):
    def body(*refs):
        len_ref, xs_hbm, gs_hbm, kv_hbm = refs[0], refs[1:4], refs[4:7], refs[7]
        q_ref, g_ref, lse_ref, delta_ref, bt_ref, a_ref = refs[8:14]
        acc2, o_acc2, dq_ref, own_ref = refs[14:17], refs[17:20], refs[20], refs[21]
        r = list(refs[22:])
        take = lambda n: [r.pop(0) for _ in range(n)]
        xs, gs, (kv_ref,) = take(3), take(3), take(1)
        sendbuf, r1a, r1b, r2, got2 = take(3), take(3), take(3), take(3), take(3)
        o_buf, o_got1, o_got2 = take(3), take(3), take(3)
        (dkv,) = take(1)
        kv1, kv2, kv3, kva1, kva2 = take(6), take(6), take(6), take(6), take(6)
        loc, send, recv = take(3)
        c = coords()
        loads = [pltpu.make_async_copy(a, b, loc.at[i]) for i, (a, b) in enumerate(
            ((xs_hbm[0], xs[0]), (gs_hbm[0], gs[0]), (xs_hbm[2], xs[2]), (gs_hbm[2], gs[2]),
             (xs_hbm[1], xs[1]), (gs_hbm[1], gs[1]), (kv_hbm, kv_ref)))]
        for copy in loads:
            copy.start()
        barrier()
        sems = iter(range(256))

        def push(src, dst, device):
            n = next(sems)
            copy = remote(src, dst, send.at[n], recv.at[n], device)
            copy.start()
            return copy

        def regroup(v, outer, inner):
            return jnp.concatenate(
                [v[(o * inner + i) * 24 : (o * inner + i + 1) * 24] for i in range(inner) for o in range(outer)], axis=0
            )

        near = lambda u: u + 1 - 2 * (u % 2)
        far = lambda u: 3 - u
        over = lambda u: (u + 2) % 4
        top, low = pl.ds(0, 192), pl.ds(192, 192)
        first, second = [[], [], []], [[], [], []]

        def neighbour(axis, u):
            return peer(axis, u + 4 - c[axis])

        def slab(m, u):
            return sendbuf[m].at[u]

        def ready(m, which):
            axis = MLP_AXES[m][1]
            u = c[axis]
            if which == "over":
                first[m].append(push(slab(m, over(u)).at[top, :], r1a[m].at[0], neighbour(axis, near(u))))
                first[m].append(push(slab(m, over(u)).at[low, :], r1b[m].at[0], neighbour(axis, far(u))))
            elif which == "near":
                first[m].append(push(slab(m, near(u)).at[top, :], r1a[m].at[1], neighbour(axis, near(u))))
            elif which == "far":
                first[m].append(push(slab(m, far(u)).at[low, :], r1b[m].at[1], neighbour(axis, far(u))))

        def second_step(m):
            axis = MLP_AXES[m][1]
            u = c[axis]
            first[m][0].wait()
            at = slab(m, far(u)).at[top, :]
            at[...] = (at[...].astype(F32) + r1a[m][0].astype(F32)).astype(BF16)
            second[m].append(push(at, r2[m].at[0], neighbour(axis, far(u))))
            first[m][1].wait()
            at = slab(m, near(u)).at[low, :]
            at[...] = (at[...].astype(F32) + r1b[m][0].astype(F32)).astype(BF16)
            second[m].append(push(at, r2[m].at[1], neighbour(axis, near(u))))

        second_axis = [[], [], []]

        def second_axis_step(m):
            axis = MLP_AXES[m][1]
            own = slab(m, c[axis])
            for copy in first[m][2:] + second[m]:
                copy.wait()
            own[top, :] = (own[top, :].astype(F32) + r1a[m][1].astype(F32) + r2[m][0].astype(F32)).astype(BF16)
            own[low, :] = (own[low, :].astype(F32) + r1b[m][1].astype(F32) + r2[m][1].astype(F32)).astype(BF16)
            axis = MLP_AXES[m][2]
            for k in (1, 2, 3):
                rows = pl.ds(pl.multiple_of(((c[axis] + k) % 4) * 96, 32), 96)
                second_axis[m].append(push(own.at[rows, :], got2[m].at[k - 1], peer(axis, k)))

        def second_axis_sum(m):
            for copy in second_axis[m]:
                copy.wait()
            rows = pl.ds(pl.multiple_of(c[MLP_AXES[m][2]] * 96, 32), 96)
            total = slab(m, c[MLP_AXES[m][1]])[rows, :].astype(F32)
            for k in range(3):
                total = total + got2[m][k].astype(F32)
            acc2[m][...] = total

        places = (("over", over), ("near", near), ("far", far), ("own", lambda u: u))
        loads[0].wait()
        loads[1].wait()
        for name, place in places:
            u = place(c["x"])
            rows = [pl.ds(pl.multiple_of(z * 384 + u * 96, 32), 96) for z in range(4)]
            x = jnp.concatenate([xs[0][r, :] for r in rows], axis=0)
            sendbuf[0][u] = regroup(mm(x, gs[0][...]), 4, 4).astype(BF16)
            ready(0, name)
        loads[2].wait()
        loads[3].wait()
        for name, place in places:
            u = place(c["z"])
            x = xs[2][pl.ds(pl.multiple_of(u * 384, 128), 384), :]
            sendbuf[2][u] = mm(x, gs[2][...]).astype(BF16)
            ready(2, name)
        loads[4].wait()
        loads[5].wait()
        for z in range(4):
            v = regroup(mm(xs[1][z * 384 : (z + 1) * 384, :], gs[1][...]), 4, 4).astype(BF16)
            for y in range(4):
                sendbuf[1][y, z * 96 : (z + 1) * 96] = v[y * 96 : (y + 1) * 96]
        for name, _ in places:
            ready(1, name)

        o_first, o_second = [[], [], []], [[], [], []]
        for p, order in enumerate(OUT_ORDERS):
            slab_products(o_buf[p], bt_ref, a_ref[:, p * 256 : (p + 1) * 256], order)
            for k in (1, 2, 3):
                there = (c[order[0]] + k) % 4
                o_first[p].append(push(o_buf[p].at[there], o_got1[p].at[k - 1], peer(order[0], k)))

        def out_second(p):
            order = OUT_ORDERS[p]
            sum_first(o_buf[p], o_got1[p], o_first[p], c[order[0]])
            for k in (1, 2, 3):
                rows = pl.ds(pl.multiple_of(((c[order[1]] + k) % 4) * 96, 32), 96)
                o_second[p].append(push(o_buf[p].at[c[order[0]], rows, :], o_got2[p].at[k - 1], peer(order[1], k)))

        def out_sum(p):
            order = OUT_ORDERS[p]
            for copy in o_second[p]:
                copy.wait()
            rows = pl.ds(pl.multiple_of(c[order[1]] * 96, 32), 96)
            total = o_buf[p][c[order[0]], rows, :].astype(F32)
            for k in range(3):
                total = total + o_got2[p][k].astype(F32)
            o_acc2[p][...] = total

        loads[6].wait()
        dev = lax.axis_index("seq")
        row = lax.broadcasted_iota(jnp.int32, (BLK, 96), 0)
        key_off = (row % Q_BLK) * 64 + row // Q_BLK
        q_off = (lax.broadcasted_iota(jnp.int32, (1, 96), 1) % Q_BLK) * 64 + dev
        dq_ref[...] = jnp.zeros_like(dq_ref)

        def k_step(kb, _):
            k_blk = kv_ref[:, kv_rows(kb, 0), :].reshape(BLK, 128)
            v_blk = kv_ref[:, kv_rows(kb, 1), :].reshape(BLK, 128)
            k_t = k_blk.T
            pos_k = key_off + kb * BLK

            def pair(qb, carry, causal):
                dk, dv = carry
                q_blk, g_blk = q_ref[qb], g_ref[qb]
                pos_q = q_off + qb * BLK
                vis = pos_k >= doc_bounds(pos_q, len_ref)
                if causal:
                    vis = vis & (pos_k <= pos_q)
                s = nt(k_blk, q_blk)
                p = jnp.where(vis, jnp.exp2(s * SCALE2 - lse_ref[qb]), 0.0)
                gp = nt(v_blk, g_blk)
                ds = (p * (gp - delta_ref[qb])).astype(BF16)
                dq_ref[qb] += mm(k_t, ds)
                dk = dk + mm(ds, q_blk)
                dv = dv + mm(p.astype(BF16), g_blk)
                return dk, dv

            zero = jnp.zeros((BLK, 128), F32)
            carry = pair(kb, (zero, zero), True)
            dk, dv = lax.fori_loop(kb + 1, 8, lambda qb, carry: pair(qb, carry, False), carry)
            dkv[:, :, :, kv_rows(kb, 0), :] = (dk * SCALE).astype(BF16).reshape(4, 4, 4, Q_BLK, 128)
            dkv[:, :, :, kv_rows(kb, 1), :] = dv.astype(BF16).reshape(4, 4, 4, Q_BLK, 128)
            return 0

        kv_pending = [[] for _ in range(6)]

        def pick1(rest, order, where):
            return (where,) if rest[0] == order[1] else (slice(None), where)

        def kv_stage(chunk, stage):
            for i, (r0, rn, order) in enumerate(KV_CHUNK):
                p, r0 = chunk * 3 + i, r0 + chunk * 128
                for copy in kv_pending[p]:
                    copy.wait()
                kv_pending[p] = []
                rest = [a for a in AXES if a not in order[:1]]
                if stage == 1:
                    own = dkv[kv_index(rest, c, r0, rn)].astype(F32)
                    for k in range(3):
                        own = own + kv1[p][k].astype(F32)
                    kva1[p][...] = own.astype(BF16)
                if stage == 2:
                    own = kva1[p][pick1(rest, order, c[order[1]])].astype(F32)
                    for k in range(3):
                        own = own + kv2[p][k].astype(F32)
                    kva2[p][...] = own.astype(BF16)
                if stage == 3:
                    own = kva2[p][c[order[2]]].astype(F32)
                    for k in range(3):
                        own = own + kv3[p][k].astype(F32)
                    own_ref[pl.ds(r0, rn), :] = own
                    continue
                for k in (1, 2, 3):
                    there = (c[order[stage]] + k) % 4
                    if stage == 0:
                        cc = dict(c)
                        cc[order[0]] = there
                        src, dst = dkv.at[kv_index(rest, cc, r0, rn)], kv1[p].at[k - 1]
                    elif stage == 1:
                        src, dst = kva1[p].at[pick1(rest, order, there)], kv2[p].at[k - 1]
                    else:
                        src, dst = kva2[p].at[there], kv3[p].at[k - 1]
                    kv_pending[p].append(push(src, dst, peer(order[stage], k)))

        lax.fori_loop(4, 8, k_step, 0)
        kv_stage(1, 0)
        second_step(0)
        lax.fori_loop(0, 1, k_step, 0)
        second_step(2)
        second_step(1)
        lax.fori_loop(1, 2, k_step, 0)
        kv_stage(1, 1)
        second_axis_step(0)
        lax.fori_loop(2, 3, k_step, 0)
        kv_stage(1, 2)
        second_axis_step(2)
        second_axis_step(1)
        for p in range(3):
            out_second(p)
        lax.fori_loop(3, 4, k_step, 0)
        kv_stage(0, 0)
        kv_stage(1, 3)
        for m in (0, 2, 1):
            second_axis_sum(m)
        for p in range(3):
            out_sum(p)
        kv_stage(0, 1)
        kv_stage(0, 2)
        kv_stage(0, 3)

    rows = [rn for _, rn, _ in KV_CHUNK] * 2
    scratch = (
        [pltpu.VMEM((1536, 512), BF16)] * 3
        + [pltpu.VMEM((512, FC), BF16)] * 3
        + [pltpu.VMEM((64, 256, 128), BF16)]
        + [pltpu.VMEM((4, 384, FC), BF16)] * 3
        + [pltpu.VMEM((2, 192, FC), BF16)] * 3
        + [pltpu.VMEM((2, 192, FC), BF16)] * 3
        + [pltpu.VMEM((2, 192, FC), BF16)] * 3
        + [pltpu.VMEM((3, 96, FC), BF16)] * 3
        + [pltpu.VMEM((4, 384, 256), BF16)] * 3
        + [pltpu.VMEM((3, 384, 256), BF16)] * 3
        + [pltpu.VMEM((3, 96, 256), BF16)] * 3
        + [pltpu.VMEM((4, 4, 4, 256, 128), BF16)]
        + [pltpu.VMEM((3, 4, 4, r, 128), BF16) for r in rows]
        + [pltpu.VMEM((3, 4, r, 128), BF16) for r in rows]
        + [pltpu.VMEM((3, r, 128), BF16) for r in rows]
        + [pltpu.VMEM((4, 4, r, 128), BF16) for r in rows]
        + [pltpu.VMEM((4, r, 128), BF16) for r in rows]
        + [DMA((7,)), DMA((128,)), DMA((128,))]
    )
    vm, sm = pl.BlockSpec(memory_space=pltpu.VMEM), pl.BlockSpec(memory_space=pltpu.SMEM)
    f32 = lambda *s: jax.ShapeDtypeStruct(s, F32)
    return pl.pallas_call(
        body,
        out_shape=(f32(96, FC),) * 3 + (f32(96, 256),) * 3 + (f32(8, 128, 96), f32(256, 128)),
        in_specs=[sm] + [pl.BlockSpec(memory_space=pl.ANY)] * 7 + [vm] * 6,
        out_specs=(vm,) * 8,
        scratch_shapes=scratch,
        compiler_params=pltpu.CompilerParams(collective_id=2, has_side_effects=True, vmem_limit_bytes=VMEM_BYTES),
        name="backward",
    )(lengths, *xs_in, *gs_in, kv, q, g, lse, delta, branch_t, attn_low)


SMALL = 40


def finish(mlp_acc, out_acc, dq_t, dkv, cos, sin, norm_t, wq, wk, wv, tokens, gain, g_mid, d_norm2):
    def body(*refs):
        late = refs[0:11]
        dq_ref, dkv_ref, cos_ref, sin_ref, nt_ref, gain_ref, dn2_ref = refs[11:18]
        gt_ref, gq_ref, gk_ref, gv_ref, go_ref, s_out = refs[18:24]
        m_outs = refs[24:27]
        r = list(refs[27:])
        take = lambda n: [r.pop(0) for _ in range(n)]
        held = take(11)
        m_acc, o_acc, (wq_ref, wk_ref, wv_ref, t_ref, gmid_ref) = held[0:3], held[3:6], held[6:11]
        m_got, o_got = take(3), take(3)
        sendbuf, got1, got2, acc2, got3 = take(3), take(3), take(3), take(3), take(3)
        s_acc, s_got, g_ref, part, got_part, loc, send, recv = take(8)
        c = coords()
        loads = [pltpu.make_async_copy(a, b, loc.at[i]) for i, (a, b) in enumerate(zip(late, held))]
        for copy in loads:
            copy.start()
        core = lax.axis_index("tensor")
        barrier(core=True)
        sems = iter(range(256))

        def push(src, dst, device):
            n = next(sems)
            copy = remote(src, dst, send.at[n], recv.at[n], device)
            copy.start()
            return copy

        def share(acc, got, axis):
            copies = []
            for k in (1, 2, 3):
                rows = pl.ds(pl.multiple_of(((c[axis] + k) % 4) * 24, 8), 24)
                copies.append(push(acc.at[rows, :], got.at[k - 1], peer(axis, k)))
            return copies

        cos_t, sin_t = cos_ref[...], sin_ref[...]
        for qb in range(8):
            dq = dq_ref[qb].T * SCALE
            rows = slice(qb * Q_BLK, (qb + 1) * Q_BLK)
            cs, sn = cos_t[rows], sin_t[rows]
            for h in range(6):
                v = dq[h * Q_BLK : (h + 1) * Q_BLK]
                g_ref[rows, h * 128 : (h + 1) * 128] = (v * cs - swap_halves(v) * sn).astype(BF16)
        dk = jnp.concatenate([dkv_ref[0:64, :], dkv_ref[128:192, :]], axis=0)
        g_ref[:, 768:896] = (dk * cos_t - swap_halves(dk) * sin_t).astype(BF16)
        g_ref[:, 896:] = jnp.concatenate([dkv_ref[64:128, :], dkv_ref[192:256, :]], axis=0).astype(BF16)

        pending = [[], [], []]
        for p, (lo, hi, order) in enumerate(QKV_PARTS):
            slab_products(sendbuf[p], nt_ref, g_ref[:, lo:hi], order)
            for k in (1, 2, 3):
                there = (c[order[0]] + k) % 4
                pending[p].append(push(sendbuf[p].at[there], got1[p].at[k - 1], peer(order[0], k)))

        for copy in loads:
            copy.wait()
        o_copies = [share(o_acc[p], o_got[p], OUT_ORDERS[p][2]) for p in range(3)]
        m_copies = [share(m_acc[m], m_got[m], MLP_AXES[m][0]) for m in range(3)]
        total = nt(g_ref[:, 768:896], wk_ref[...]) + nt(g_ref[:, 896:], wv_ref[...])
        for h in range(6):
            total = total + nt(g_ref[:, h * 128 : (h + 1) * 128], wq_ref[h])
        part[...] = total
        swap = push(part, got_part, partner())

        inputs = t_ref[...].astype(F32)
        inv = lax.rsqrt(jnp.mean(inputs * inputs, axis=1, keepdims=True) + 1e-06)
        d_norm1 = jnp.sum(part[...] * inputs * inv, axis=0, keepdims=True)
        d_bias = jnp.sum(g_ref[...].astype(F32), axis=0, keepdims=True)
        for j in range(12):
            s_acc[0, j : j + 1, :] = d_norm1[:, j * 128 : (j + 1) * 128]
            s_acc[0, 12 + j : 13 + j, :] = dn2_ref[:, j * 128 : (j + 1) * 128]
        for j in range(8):
            v = d_bias[:, j * 128 : (j + 1) * 128]
            s_acc[0, 24 + j : 25 + j, :] = jnp.where(core == 0, v, 0.0)
            s_acc[0, 32 + j : 33 + j, :] = jnp.where(core == 1, v, 0.0)
        s_pending = []

        def send_small(stage):
            peers = [partner()] if stage == 0 else [peer(AXES[stage - 1], k) for k in (1, 2, 3)]
            for i, d in enumerate(peers):
                s_pending.append(push(s_acc.at[stage], s_got.at[stage * 3 + i], d))

        def sum_small(stage):
            for copy in s_pending:
                copy.wait()
            s_pending.clear()
            if stage == 0:
                return s_acc[0] + s_got[0]
            axis = AXES[stage - 1]
            parts = [s_acc[stage]] + [s_got[stage * 3 + k] for k in range(3)]
            total = jnp.zeros_like(parts[0])
            for w in range(4):
                term = jnp.zeros_like(total)
                for k in range(4):
                    term = jnp.where((c[axis] + 4 - k) % 4 == w, parts[k], term)
                total = total + term
            return total

        send_small(0)
        for p in range(3):
            for copy in o_copies[p]:
                copy.wait()
            rows = pl.ds(pl.multiple_of(c[OUT_ORDERS[p][2]] * 24, 8), 24)
            total = o_acc[p][rows, :]
            for k in range(3):
                total = total + o_got[p][k]
            for j in range(2):
                go_ref[p * 2 + j] = total[:, j * 128 : (j + 1) * 128]
        s_acc[1] = sum_small(0)
        send_small(1)
        swap.wait()
        g_norm = part[...] + got_part[...]
        scaled = g_norm * gain_ref[0:1, :]
        gt_ref[...] = gmid_ref[...] + (
            inv * scaled - inputs * (inv * inv * inv) * jnp.mean(scaled * inputs, axis=1, keepdims=True)
        )
        for p, (lo, hi, order) in enumerate(QKV_PARTS):
            own = c[order[0]]
            sum_first(sendbuf[p], got1[p], pending[p], own)
            pending[p] = []
            for k in (1, 2, 3):
                rows = pl.ds(pl.multiple_of(((c[order[1]] + k) % 4) * 96, 32), 96)
                pending[p].append(push(sendbuf[p].at[own, rows, :], got2[p].at[k - 1], peer(order[1], k)))
        s_acc[2] = sum_small(1)
        send_small(2)
        for m in range(3):
            for copy in m_copies[m]:
                copy.wait()
            here = c[MLP_AXES[m][0]]
            m_outs[m][:, pl.ds(col_start(here), FC)] = m_acc[m][pl.ds(pl.multiple_of(here * 24, 8), 24), :]
            for k in (1, 2, 3):
                m_outs[m][:, pl.ds(col_start((here + 4 - k) % 4), FC)] = m_got[m][k - 1]
        for p, (lo, hi, order) in enumerate(QKV_PARTS):
            for copy in pending[p]:
                copy.wait()
            own = c[order[0]]
            rows = pl.ds(pl.multiple_of(c[order[1]] * 96, 32), 96)
            total = sendbuf[p][own, rows, :].astype(F32)
            for k in range(3):
                total = total + got2[p][k].astype(F32)
            acc2[p][...] = total
            pending[p] = share(acc2[p], got3[p], order[2])
        s_acc[3] = sum_small(2)
        send_small(3)
        for p, (lo, hi, order) in enumerate(QKV_PARTS):
            for copy in pending[p]:
                copy.wait()
            rows = pl.ds(pl.multiple_of(c[order[2]] * 24, 8), 24)
            total = acc2[p][rows, :]
            for k in range(3):
                total = total + got3[p][k]
            for j in range(lo // 128, hi // 128):
                v = total[:, j * 128 - lo : (j + 1) * 128 - lo]
                if j < 6:
                    gq_ref[j] = v
                elif j == 6:
                    gk_ref[...] = v
                else:
                    gv_ref[...] = v
        s_out[...] = sum_small(3)

    cols = [hi - lo for lo, hi, _ in QKV_PARTS]
    late = (*mlp_acc, *out_acc, wq, wk, wv, tokens, g_mid)
    scratch = (
        [pltpu.VMEM(v.shape, v.dtype) for v in late]
        + [pltpu.VMEM((3, 24, FC), F32)] * 3
        + [pltpu.VMEM((3, 24, 256), F32)] * 3
        + [pltpu.VMEM((4, 384, n), BF16) for n in cols]
        + [pltpu.VMEM((3, 384, n), BF16) for n in cols]
        + [pltpu.VMEM((3, 96, n), BF16) for n in cols]
        + [pltpu.VMEM((96, n), F32) for n in cols]
        + [pltpu.VMEM((3, 24, n), F32) for n in cols]
        + [
            pltpu.VMEM((4, SMALL, 128), F32),
            pltpu.VMEM((12, SMALL, 128), F32),
            pltpu.VMEM((128, 1024), BF16),
            pltpu.VMEM((128, 1536), F32),
            pltpu.VMEM((128, 1536), F32),
            DMA((11,)),
            DMA((64,)),
            DMA((64,)),
        ]
    )
    f32 = lambda *s: jax.ShapeDtypeStruct(s, F32)
    shape = (f32(128, 1536), f32(6, 24, 128), f32(24, 128), f32(24, 128), f32(6, 24, 128), f32(SMALL, 128))
    shape = shape + (f32(24, 4480),) * 3
    vm, hbm = pl.BlockSpec(memory_space=pltpu.VMEM), pl.BlockSpec(memory_space=pl.ANY)
    return pl.pallas_call(
        body,
        out_shape=shape,
        in_specs=[hbm] * 11 + [vm] * 7,
        out_specs=(vm,) * 9,
        scratch_shapes=scratch,
        compiler_params=pltpu.CompilerParams(collective_id=3, has_side_effects=True, vmem_limit_bytes=VMEM_BYTES),
        name="finish",
    )(*late, dq_t, dkv, cos, sin, norm_t, gain, d_norm2)


def hand_out(*arrays):
    n = len(arrays)

    def body(*refs):
        ins, outs, sem = refs[:n], refs[n : 2 * n], refs[2 * n]
        copies = [pltpu.make_async_copy(a, b, sem.at[i]) for i, (a, b) in enumerate(zip(ins, outs))]
        for copy in copies:
            copy.start()
        for copy in copies:
            copy.wait()

    hbm = pl.BlockSpec(memory_space=pl.ANY)
    return pl.pallas_call(
        body,
        out_shape=tuple(jax.ShapeDtypeStruct(v.shape, v.dtype) for v in arrays),
        in_specs=[hbm] * n,
        out_specs=(hbm,) * n,
        scratch_shapes=[DMA((n,))],
        name="hand_out",
    )(*arrays)


def local(
    tokens, cotangent, lengths, norm1_gain, w_query, b_query, w_key, b_key, w_value, b_value, w_out,
    norm2_gain, w_gate, w_up, w_down,
):
    device = lax.axis_index("seq")
    core = lax.axis_index("tensor")
    wq = w_query.transpose(1, 0, 2)
    wk, wv = w_key.reshape(1536, 128), w_value.reshape(1536, 128)
    wo = w_out.reshape(768, 1536)
    gains = jnp.stack([norm1_gain, norm2_gain])

    q, kv, norm_t, cos, sin = qkv_gather(tokens, gains, wq, wk, wv, b_query, b_key, b_value, lengths)
    kv = kv.reshape(64, 256, 128)
    branch, attn, attn_low, lse = attn_forward(q, kv, wo, lengths)
    output, g_mid, branch_t, g_attn, delta, d_norm2, *shared = feed_forward(
        branch, attn, tokens, cotangent, gains, wo, w_gate, w_up, w_down
    )
    *acc, dq_t, dkv = backward(shared[:3], shared[3:], q, g_attn, kv, lse, delta, branch_t, attn_low, lengths)
    grad_tokens, grad_wq, grad_wk, grad_wv, grad_wo, sums, grad_gate, grad_up, grad_down = finish(
        acc[:3], acc[3:], dq_t, dkv, cos, sin, norm_t, wq, wk, wv, tokens, gains, g_mid, d_norm2
    )
    output, grad_tokens, grad_wq, grad_wk, grad_wv, grad_wo, grad_gate, grad_up, grad_down = hand_out(
        output, grad_tokens, grad_wq, grad_wk, grad_wv, grad_wo, grad_gate, grad_up, grad_down
    )
    sums = sums.reshape(-1)
    grad_norm1 = lax.dynamic_slice(sums, (device * 24,), (24,))
    grad_norm2 = lax.dynamic_slice(sums, (1536 + device * 24,), (24,))
    bias = lax.dynamic_slice(sums.reshape(SMALL, 128), (24 + core * 8, device * 2), (8, 2))
    return (
        output,
        grad_tokens,
        grad_norm1,
        grad_wq.transpose(1, 0, 2),
        bias[:6],
        grad_wk.reshape(24, 1, 128),
        bias[6:7],
        grad_wv.reshape(24, 1, 128),
        bias[7:8],
        grad_wo.transpose(0, 2, 1),
        grad_norm2,
        grad_gate,
        grad_up,
        grad_down.T,
    )


def solution(mesh):
    in_specs = (
        P("seq", None), P("seq", None), P(), P(), P(None, "tensor", None), P("tensor", None),
        P(None, "tensor", None), P("tensor", None), P(None, "tensor", None), P("tensor", None),
        P("tensor", None, None), P(), P(None, "tensor"), P(None, "tensor"), P("tensor", None),
    )
    out_specs = (
        P("seq", None), P("seq", None), P("seq"), P("seq", "tensor", None), P("tensor", "seq"),
        P("seq", "tensor", None), P("tensor", "seq"), P("seq", "tensor", None), P("tensor", "seq"),
        P("tensor", None, "seq"), P("seq"), P("seq", "tensor"), P("seq", "tensor"), P("tensor", "seq"),
    )
    return jax.shard_map(local, mesh=mesh, in_specs=in_specs, out_specs=out_specs, check_vma=False)
```

profile of v0, /device:TPU:0, one launch (start us, length us, event | category | flops | bytes accessed | tf_op | source)
XLA Modules:
  0.0 324.8 jit_solution(8531555536705899647)
XLA Ops:
  0.6 0.7 stack.10
  1.3 0.7 stack.9
  2.0 0.6 pad_maximum_fusion.g_ref.refs_16_
  2.7 37.8 %qkv_gather.1 = (bf16[8,96,128]{2,1,0:T(8,128)(2,1)}, bf16[4,4,4,256,128]{4,3,2,1,0:T(8,128)(2,1)}, bf16[1536,128]{1,0:T(8,128)(2,1)}, f32[128,128]{1,0:T(8,128)}, f32[128,128]{1,0:T(8,128)}) custom-call(s32[8]{0:T(128)} %refs_0_.1, bf16[128,1536]{1,0:T(8,128)(2,1)} %refs_9_.1, f32[2,1536]{1,0:T(2,128)} %pad_maximum_fusion.g_ref.refs_16_, ...), custom_call_target="tpu_custom_call" | custom-call | tf_op jit(solution)/shard_map/qkv_gather/pallas_call | solution.py:127
  40.5 16.3 %attn_forward.1 = (f32[128,1536]{1,0:T(8,128)}, f32[8,96,128]{2,1,0:T(8,128)}, bf16[128,768]{1,0:T(8,128)(2,1)}, f32[8,1,96]{2,1,0:T(1,128)}) custom-call(s32[8]{0:T(128)} %refs_0_.1, bf16[8,96,128]{2,1,0:T(8,128)(2,1)} %get-tuple-element.61.q_ref.refs_8_, bf16[64,256,128]{2,1,0:T(8,128)(2,1)} %bitcast.16, bf16[768,1536]{1,0:T(8,128)(2,1)} %bitcast.18), custom_call_target="tpu_custom_call" | custom-call | tf_op jit(solution)/shard_map/attn_forward/pallas_call | solution.py:221
  56.8 41.0 %feed_forward.1 = (f32[128,1536]{1,0:T(8,128)}, f32[128,1536]{1,0:T(8,128)}, bf16[1536,128]{1,0:T(8,128)(2,1)}, bf16[8,96,128]{2,1,0:T(8,128)(2,1)}, f32[8,1,96]...) custom-call(f32[128,1536]{1,0:T(8,128)} %get-tuple-element.63.br_ref, ...), custom_call_target="tpu_custom_call" | custom-call | tf_op jit(solution)/shard_map/feed_forward/pallas_call | solution.py:390
  97.8 94.4 %backward.1 = (f32[96,1152]{1,0:T(8,128)}, f32[96,1152]{1,0:T(8,128)}, f32[96,1152]{1,0:T(8,128)}, f32[96,256]{1,0:T(8,128)}, f32[96,256]{1,0:T(8,128)}, /*index...) custom-call(s32[8]{0:T(128)} %refs_0_.1, bf16[1536,512]{1,0:T(8,128)(2,1)} %get-tuple-element.66.refs_1_, ...), custom_call_target="tpu_custom_call" | custom-call | tf_op jit(solution)/shard_map/backward/pallas_call | solution.py:717
  192.2 36.0 %finish.1 = (f32[128,1536]{1,0:T(8,128)}, f32[6,24,128]{2,1,0:T(8,128)}, f32[24,128]{1,0:T(8,128)}, f32[24,128]{1,0:T(8,128)}, f32[6,24,128]{2,1,0:T(8,128)}, /*...) custom-call(f32[96,1152]{1,0:T(8,128)} %get-tuple-element.77.refs_0_, ...), custom_call_target="tpu_custom_call" | custom-call | tf_op jit(solution)/shard_map/finish/pallas_call | solution.py:917
  228.2 93.1 %hand_out.1 = (f32[128,1536]{1,0:T(8,128)}, f32[128,1536]{1,0:T(8,128)}, f32[6,24,128]{2,1,0:T(8,128)}, f32[24,128]{1,0:T(8,128)}, f32[24,128]{1,0:T(8,128)}, /*...) custom-call(f32[128,1536]{1,0:T(8,128)} %get-tuple-element.65.refs_0_, ...), custom_call_target="tpu_custom_call" | custom-call | tf_op jit(solution)/shard_map/hand_out/pallas_call | solution.py:940
  321.4 0.8 dynamic_slice.10
  322.1 0.5 fusion.1
  322.6 0.6 copy.29
  323.3 1.4 fusion
where the time goes:
time: 328 us; the launch traced here: 325 us
  Pallas kernels  319 us (97%)
  local copies, waits for them, and re-layouts  4.68 us (1%)
    pallas_call x1, Pallas kernels, backward(): pl.pallas_call(body, out_shape=(f32(96, FC),) * 3 + (f32(96, 256),) * 3 +...  94.4 us
    pallas_call x1, Pallas kernels, hand_out(): pl.pallas_call(body, out_shape=tuple((jax.ShapeDtypeStruct(v.shape, v.dty...  93.1 us
    pallas_call x1, Pallas kernels, feed_forward(): pl.pallas_call(body, out_shape=(f32(128, 1536), f32(128, 1536), b16(1536,...  41 us
    pallas_call x1, Pallas kernels, qkv_gather(): pl.pallas_call(body, out_shape=(jax.ShapeDtypeStruct((8, 96, 128), BF16),...  37.8 us
    pallas_call x1, Pallas kernels, finish(): pl.pallas_call(body, out_shape=shape, in_specs=[hbm] * 11 + [vm] * 7, out...  36 us
    pallas_call x1, Pallas kernels, attn_forward(): pl.pallas_call(body, out_shape=(jax.ShapeDtypeStruct((128, 1536), F32), j...  16.3 us

commit v1 on v0

--- a/solution.py
+++ b/solution.py
@@ -252,6 +252,17 @@
 MLP_AXES = (("z", "x", "y"), ("x", "y", "z"), ("y", "z", "x"))
 
 
+def in_order(v, order):
+    place = {}
+    rows = []
+    for i in range(64):
+        for n, a in enumerate(order):
+            place[a] = (i // (16, 4, 1)[n]) % 4
+        o = place["z"] * 16 + place["x"] * 4 + place["y"]
+        rows.append(v[o * 24 : (o + 1) * 24])
+    return jnp.concatenate(rows, axis=0)
+
+
 def feed_forward(branch, attn, tokens, cot, gain, w_out, w_gate, w_up, w_down):
     def body(br_ref, at_ref, t_ref, c_ref, g_ref, wo_hbm, wg_hbm, wu_hbm, wd_hbm,
              out_ref, gmid_ref, bt_ref, ga_ref, delta_ref, dn_ref, x0, x1, x2, g0, g1, g2,
@@ -284,26 +295,28 @@
 
         later = []
         ex = push(br_ref, got_br, partner())
-        ct_ref[...] = c_ref[...].T
-        own = [pltpu.make_async_copy(ct_ref, x2.at[:, pl.ds(0, 128)], loc.at[3])]
+        ct_ref[...] = c_ref[...].T.reshape(4, 384, 128)
+        own = [pltpu.make_async_copy(ct_ref, x2.at[:, :, pl.ds(0, 128)], loc.at[3])]
         own[0].start()
         for k in (1, 2, 3):
-            later.append(push(ct_ref, x2.at[:, pl.ds(k * 128, 128)], peer("y", k)))
+            later.append(push(ct_ref, x2.at[:, :, pl.ds(k * 128, 128)], peer("y", k)))
         ex.wait()
         mid = t_ref[...].astype(F32) + (br_ref[...] + got_br[...])
         mid_ref[...] = mid
         inv = lax.rsqrt(jnp.mean(mid * mid, axis=1, keepdims=True) + 1e-06)
         normed = (mid * inv * g_ref[1:2, :]).astype(BF16)
         norm_ref[...] = normed
-        nt_ref[...] = normed.T
-        own.append(pltpu.make_async_copy(nt_ref, x0.at[:, pl.ds(0, 128)], loc.at[4]))
-        own.append(pltpu.make_async_copy(nt_ref, x1.at[:, pl.ds(0, 128)], loc.at[5]))
+        turned = normed.astype(F32).T
+        for m in range(2):
+            nt_ref[m] = in_order(turned, MLP_AXES[m][1:] + MLP_AXES[m][:1]).astype(BF16).reshape(4, 384, 128)
+        own.append(pltpu.make_async_copy(nt_ref.at[0], x0.at[:, :, pl.ds(0, 128)], loc.at[4]))
+        own.append(pltpu.make_async_copy(nt_ref.at[1], x1.at[:, :, pl.ds(0, 128)], loc.at[5]))
         own.append(pltpu.make_async_copy(wo_hbm, wo_ref, loc.at[6]))
         for copy in own[1:]:
             copy.start()
         for k in (1, 2, 3):
             for m, w in ((0, "z"), (1, "x")):
-                later.append(push(nt_ref, xs[m].at[:, pl.ds(k * 128, 128)], peer(w, k)))
+                later.append(push(nt_ref.at[m], xs[m].at[:, :, pl.ds(k * 128, 128)], peer(w, k)))
 
         lane = lax.broadcasted_iota(jnp.int32, (128, FC), 1)
         for j in range(4):
@@ -390,7 +403,7 @@
     return pl.pallas_call(
         body,
         out_shape=(f32(128, 1536), f32(128, 1536), b16(1536, 128), b16(8, 96, 128), f32(8, 1, 96), f32(1, 1536))
-        + (b16(1536, 512),) * 3
+        + (b16(4, 384, 512),) * 3
         + (b16(512, FC),) * 3,
         in_specs=[vm] * 5 + [hbm] * 4,
         out_specs=(vm,) * 6 + (hbm,) * 6,
@@ -404,8 +417,8 @@
             pltpu.VMEM((2, 128, 1536), F32),
             pltpu.VMEM((128, 1536), F32),
             pltpu.VMEM((128, 1536), BF16),
-            pltpu.VMEM((1536, 128), BF16),
-            pltpu.VMEM((1536, 128), BF16),
+            pltpu.VMEM((2, 4, 384, 128), BF16),
+            pltpu.VMEM((4, 384, 128), BF16),
             pltpu.VMEM((3, 4, 128, FC), BF16),
             DMA((2, 3)),
             DMA((7,)),
@@ -418,7 +431,14 @@
 
 
 OUT_ORDERS = (("z", "x", "y"), ("x", "y", "z"), ("y", "z", "x"))
-QKV_PARTS = ((0, 384, ("z", "x", "y")), (384, 768, ("x", "y", "z")), (768, 1024, ("y", "z", "x")))
+QKV_PARTS = (
+    (0, 256, ("z", "x", "y")),
+    (256, 512, ("x", "y", "z")),
+    (512, 768, ("y", "z", "x")),
+    (768, 896, ("z", "x", "y")),
+    (896, 1024, ("x", "y", "z")),
+)
+SMALL = 40
 
 
 def slab_products(buf, left, rhs, order):
@@ -445,30 +465,44 @@
         copy.wait()
     total = buf[own].astype(F32)
     for k in range(3):
-        total = total + got[k].astype(F32)
+        total = total + got[k][...].astype(F32)
     buf[own] = total.astype(BF16)
 
 
-def backward(xs_in, gs_in, q, g, kv, lse, delta, branch_t, attn_low, lengths):
+def backward(xs_in, gs_in, q, g, kv, lse, delta, branch_t, attn_low, lengths,
+             cos, sin, norm_t, wq, wk, wv, tokens, gain, g_mid, d_norm2):
+    n_late = 2
+
     def body(*refs):
-        len_ref, xs_hbm, gs_hbm, kv_hbm = refs[0], refs[1:4], refs[4:7], refs[7]
-        q_ref, g_ref, lse_ref, delta_ref, bt_ref, a_ref = refs[8:14]
-        acc2, o_acc2, dq_ref, own_ref = refs[14:17], refs[17:20], refs[20], refs[21]
-        r = list(refs[22:])
+        r = list(refs)
         take = lambda n: [r.pop(0) for _ in range(n)]
-        xs, gs, (kv_ref,) = take(3), take(3), take(1)
+        (len_ref,), xs_hbm, gs_hbm, (kv_hbm, *w_hbm), late = take(1), take(3), take(3), take(4), take(n_late)
+        q_ref, g_ref, lse_ref, delta_ref, bt_ref, a_ref, cos_ref, sin_ref, nt_ref, gain_ref, dn2_ref = take(11)
+        gt_ref, gq_ref, gk_ref, gv_ref, go_ref, s_out = take(6)
+        m_outs = take(3)
+        xs, gs, (dkv,), (t_ref,) = take(3), take(3), take(1), take(1)
+        held = (t_ref, gt_ref)
+        acc2, o_acc2, (dq_ref, own_ref) = take(3), take(3), take(2)
         sendbuf, r1a, r1b, r2, got2 = take(3), take(3), take(3), take(3), take(3)
-        o_buf, o_got1, o_got2 = take(3), take(3), take(3)
-        (dkv,) = take(1)
-        kv1, kv2, kv3, kva1, kva2 = take(6), take(6), take(6), take(6), take(6)
+        o_buf, o_got1, o_got2 = take(1), take(3), take(3)
+        kv1, kv2, kv3 = take(6), take(6), take(6)
+        m_got, o_got = take(3), take(3)
+        n_parts = len(QKV_PARTS)
+        q_got2, q_acc2, q_got3 = (take(n_parts) for _ in range(3))
+        o_buf = [xs[2].at[:, :, 0:256], xs[2].at[:, :, 256:512], o_buf[0]]
+        room = ((0, 0, 256), (0, 256, 512), (1, 0, 256), (1, 256, 384), (1, 384, 512))
+        q_buf = [xs[m].at[:, :, lo:hi] for m, lo, hi in room]
+        room = ((0, 0, 256), (1, 0, 256), (2, 0, 256), (0, 768, 128), (1, 768, 128))
+        q_got1 = [[gs[m].at[0:384, lo + k * n : lo + (k + 1) * n] for k in range(3)] for m, lo, n in room]
+        s_acc, s_got, gp_ref, part, got_part = take(5)
         loc, send, recv = take(3)
         c = coords()
         loads = [pltpu.make_async_copy(a, b, loc.at[i]) for i, (a, b) in enumerate(
             ((xs_hbm[0], xs[0]), (gs_hbm[0], gs[0]), (xs_hbm[2], xs[2]), (gs_hbm[2], gs[2]),
-             (xs_hbm[1], xs[1]), (gs_hbm[1], gs[1]), (kv_hbm, kv_ref)))]
+             (xs_hbm[1], xs[1]), (gs_hbm[1], gs[1]), (kv_hbm, dkv), *zip(late, held)))]
         for copy in loads:
             copy.start()
-        barrier()
+        barrier(core=True)
         sems = iter(range(256))
 
         def push(src, dst, device):
@@ -476,11 +510,6 @@
             copy = remote(src, dst, send.at[n], recv.at[n], device)
             copy.start()
             return copy
-
-        def regroup(v, outer, inner):
-            return jnp.concatenate(
-                [v[(o * inner + i) * 24 : (o * inner + i + 1) * 24] for i in range(inner) for o in range(outer)], axis=0
-            )
 
         near = lambda u: u + 1 - 2 * (u % 2)
         far = lambda u: 3 - u
@@ -540,33 +569,19 @@
                 total = total + got2[m][k].astype(F32)
             acc2[m][...] = total
 
-        places = (("over", over), ("near", near), ("far", far), ("own", lambda u: u))
-        loads[0].wait()
-        loads[1].wait()
-        for name, place in places:
-            u = place(c["x"])
-            rows = [pl.ds(pl.multiple_of(z * 384 + u * 96, 32), 96) for z in range(4)]
-            x = jnp.concatenate([xs[0][r, :] for r in rows], axis=0)
-            sendbuf[0][u] = regroup(mm(x, gs[0][...]), 4, 4).astype(BF16)
-            ready(0, name)
-        loads[2].wait()
-        loads[3].wait()
-        for name, place in places:
-            u = place(c["z"])
-            x = xs[2][pl.ds(pl.multiple_of(u * 384, 128), 384), :]
-            sendbuf[2][u] = mm(x, gs[2][...]).astype(BF16)
-            ready(2, name)
-        loads[4].wait()
-        loads[5].wait()
-        for z in range(4):
-            v = regroup(mm(xs[1][z * 384 : (z + 1) * 384, :], gs[1][...]), 4, 4).astype(BF16)
-            for y in range(4):
-                sendbuf[1][y, z * 96 : (z + 1) * 96] = v[y * 96 : (y + 1) * 96]
-        for name, _ in places:
-            ready(1, name)
+        for name, place in (("over", over), ("near", near), ("far", far), ("own", lambda u: u)):
+            for i, m in enumerate((0, 2, 1)):
+                if name == "over":
+                    loads[2 * i].wait()
+                    loads[2 * i + 1].wait()
+                u = place(c[MLP_AXES[m][1]])
+                x = xs[m][u]
+                sendbuf[m][u] = mm(x, gs[m][...]).astype(BF16)
+                ready(m, name)
 
         o_first, o_second = [[], [], []], [[], [], []]
-        for p, order in enumerate(OUT_ORDERS):
+        def out_first(p):
+            order = OUT_ORDERS[p]
             slab_products(o_buf[p], bt_ref, a_ref[:, p * 256 : (p + 1) * 256], order)
             for k in (1, 2, 3):
                 there = (c[order[0]] + k) % 4
@@ -574,7 +589,7 @@
 
         def out_second(p):
             order = OUT_ORDERS[p]
-            sum_first(o_buf[p], o_got1[p], o_first[p], c[order[0]])
+            sum_first(o_buf[p], [o_got1[p].at[k] for k in range(3)], o_first[p], c[order[0]])
             for k in (1, 2, 3):
                 rows = pl.ds(pl.multiple_of(((c[order[1]] + k) % 4) * 96, 32), 96)
                 o_second[p].append(push(o_buf[p].at[c[order[0]], rows, :], o_got2[p].at[k - 1], peer(order[1], k)))
@@ -597,8 +612,8 @@
         dq_ref[...] = jnp.zeros_like(dq_ref)
 
         def k_step(kb, _):
-            k_blk = kv_ref[:, kv_rows(kb, 0), :].reshape(BLK, 128)
-            v_blk = kv_ref[:, kv_rows(kb, 1), :].reshape(BLK, 128)
+            k_blk = dkv[:, :, :, kv_rows(kb, 0), :].reshape(BLK, 128)
+            v_blk = dkv[:, :, :, kv_rows(kb, 1), :].reshape(BLK, 128)
             k_t = k_blk.T
             pos_k = key_off + kb * BLK
 
@@ -627,43 +642,79 @@
 
         kv_pending = [[] for _ in range(6)]
 
-        def pick1(rest, order, where):
-            return (where,) if rest[0] == order[1] else (slice(None), where)
-
         def kv_stage(chunk, stage):
             for i, (r0, rn, order) in enumerate(KV_CHUNK):
                 p, r0 = chunk * 3 + i, r0 + chunk * 128
                 for copy in kv_pending[p]:
                     copy.wait()
                 kv_pending[p] = []
-                rest = [a for a in AXES if a not in order[:1]]
-                if stage == 1:
-                    own = dkv[kv_index(rest, c, r0, rn)].astype(F32)
+                got = (kv1, kv2, kv3)
+                if stage:
+                    mine = kv_index(order[stage:], c, r0, rn)
+                    own = dkv[mine].astype(F32)
                     for k in range(3):
-                        own = own + kv1[p][k].astype(F32)
-                    kva1[p][...] = own.astype(BF16)
-                if stage == 2:
-                    own = kva1[p][pick1(rest, order, c[order[1]])].astype(F32)
-                    for k in range(3):
-                        own = own + kv2[p][k].astype(F32)
-                    kva2[p][...] = own.astype(BF16)
-                if stage == 3:
-                    own = kva2[p][c[order[2]]].astype(F32)
-                    for k in range(3):
-                        own = own + kv3[p][k].astype(F32)
-                    own_ref[pl.ds(r0, rn), :] = own
-                    continue
+                        own = own + got[stage - 1][p][k].astype(F32)
+                    if stage == 3:
+                        own_ref[pl.ds(r0, rn), :] = own
+                        continue
+                    dkv[mine] = own.astype(BF16)
                 for k in (1, 2, 3):
                     there = (c[order[stage]] + k) % 4
-                    if stage == 0:
-                        cc = dict(c)
-                        cc[order[0]] = there
-                        src, dst = dkv.at[kv_index(rest, cc, r0, rn)], kv1[p].at[k - 1]
-                    elif stage == 1:
-                        src, dst = kva1[p].at[pick1(rest, order, there)], kv2[p].at[k - 1]
-                    else:
-                        src, dst = kva2[p].at[there], kv3[p].at[k - 1]
-                    kv_pending[p].append(push(src, dst, peer(order[stage], k)))
+                    cc = dict(c)
+                    cc[order[stage]] = there
+                    src = dkv.at[kv_index(order[stage + 1 :], cc, r0, rn)]
+                    kv_pending[p].append(push(src, got[stage][p].at[k - 1], peer(order[stage], k)))
+
+        def share(acc, got, axis):
+            copies = []
+            for k in (1, 2, 3):
+                rows = pl.ds(pl.multiple_of(((c[axis] + k) % 4) * 24, 8), 24)
+                copies.append(push(acc.at[rows, :], got.at[k - 1], peer(axis, k)))
+            return copies
+
+        q_copies = [[] for _ in QKV_PARTS]
+
+        def qkv_first(p):
+            lo, hi, order = QKV_PARTS[p]
+            slab_products(q_buf[p], nt_ref, gp_ref[:, lo:hi], order)
+            for k in (1, 2, 3):
+                there = (c[order[0]] + k) % 4
+                q_copies[p].append(push(q_buf[p].at[there], q_got1[p][k - 1], peer(order[0], k)))
+
+        def qkv_second(p):
+            order = QKV_PARTS[p][2]
+            sum_first(q_buf[p], q_got1[p], q_copies[p], c[order[0]])
+            q_copies[p] = []
+            for k in (1, 2, 3):
+                rows = pl.ds(pl.multiple_of(((c[order[1]] + k) % 4) * 96, 32), 96)
+                q_copies[p].append(push(q_buf[p].at[c[order[0]], rows, :], q_got2[p].at[k - 1], peer(order[1], k)))
+
+        def qkv_third(p):
+            order = QKV_PARTS[p][2]
+            for copy in q_copies[p]:
+                copy.wait()
+            rows = pl.ds(pl.multiple_of(c[order[1]] * 96, 32), 96)
+            total = q_buf[p][c[order[0]], rows, :].astype(F32)
+            for k in range(3):
+                total = total + q_got2[p][k].astype(F32)
+            q_acc2[p][...] = total
+            q_copies[p] = share(q_acc2[p], q_got3[p], order[2])
+
+        def qkv_out(p):
+            lo, hi, order = QKV_PARTS[p]
+            for copy in q_copies[p]:
+                copy.wait()
+            total = q_acc2[p][pl.ds(pl.multiple_of(c[order[2]] * 24, 8), 24), :]
+            for k in range(3):
+                total = total + q_got3[p][k]
+            for j in range(lo // 128, hi // 128):
+                v = total[:, j * 128 - lo : (j + 1) * 128 - lo]
+                if j < 6:
+                    gq_ref[j] = v
+                elif j == 6:
+                    gk_ref[...] = v
+                else:
+                    gv_ref[...] = v
 
         lax.fori_loop(4, 8, k_step, 0)
         kv_stage(1, 0)
@@ -674,93 +725,14 @@
         lax.fori_loop(1, 2, k_step, 0)
         kv_stage(1, 1)
         second_axis_step(0)
+        for p in range(3):
+            out_first(p)
         lax.fori_loop(2, 3, k_step, 0)
         kv_stage(1, 2)
         second_axis_step(2)
         second_axis_step(1)
-        for p in range(3):
-            out_second(p)
         lax.fori_loop(3, 4, k_step, 0)
         kv_stage(0, 0)
-        kv_stage(1, 3)
-        for m in (0, 2, 1):
-            second_axis_sum(m)
-        for p in range(3):
-            out_sum(p)
-        kv_stage(0, 1)
-        kv_stage(0, 2)
-        kv_stage(0, 3)
-
-    rows = [rn for _, rn, _ in KV_CHUNK] * 2
-    scratch = (
-        [pltpu.VMEM((1536, 512), BF16)] * 3
-        + [pltpu.VMEM((512, FC), BF16)] * 3
-        + [pltpu.VMEM((64, 256, 128), BF16)]
-        + [pltpu.VMEM((4, 384, FC), BF16)] * 3
-        + [pltpu.VMEM((2, 192, FC), BF16)] * 3
-        + [pltpu.VMEM((2, 192, FC), BF16)] * 3
-        + [pltpu.VMEM((2, 192, FC), BF16)] * 3
-        + [pltpu.VMEM((3, 96, FC), BF16)] * 3
-        + [pltpu.VMEM((4, 384, 256), BF16)] * 3
-        + [pltpu.VMEM((3, 384, 256), BF16)] * 3
-        + [pltpu.VMEM((3, 96, 256), BF16)] * 3
-        + [pltpu.VMEM((4, 4, 4, 256, 128), BF16)]
-        + [pltpu.VMEM((3, 4, 4, r, 128), BF16) for r in rows]
-        + [pltpu.VMEM((3, 4, r, 128), BF16) for r in rows]
-        + [pltpu.VMEM((3, r, 128), BF16) for r in rows]
-        + [pltpu.VMEM((4, 4, r, 128), BF16) for r in rows]
-        + [pltpu.VMEM((4, r, 128), BF16) for r in rows]
-        + [DMA((7,)), DMA((128,)), DMA((128,))]
-    )
-    vm, sm = pl.BlockSpec(memory_space=pltpu.VMEM), pl.BlockSpec(memory_space=pltpu.SMEM)
-    f32 = lambda *s: jax.ShapeDtypeStruct(s, F32)
-    return pl.pallas_call(
-        body,
-        out_shape=(f32(96, FC),) * 3 + (f32(96, 256),) * 3 + (f32(8, 128, 96), f32(256, 128)),
-        in_specs=[sm] + [pl.BlockSpec(memory_space=pl.ANY)] * 7 + [vm] * 6,
-        out_specs=(vm,) * 8,
-        scratch_shapes=scratch,
-        compiler_params=pltpu.CompilerParams(collective_id=2, has_side_effects=True, vmem_limit_bytes=VMEM_BYTES),
-        name="backward",
-    )(lengths, *xs_in, *gs_in, kv, q, g, lse, delta, branch_t, attn_low)
-
-
-SMALL = 40
-
-
-def finish(mlp_acc, out_acc, dq_t, dkv, cos, sin, norm_t, wq, wk, wv, tokens, gain, g_mid, d_norm2):
-    def body(*refs):
-        late = refs[0:11]
-        dq_ref, dkv_ref, cos_ref, sin_ref, nt_ref, gain_ref, dn2_ref = refs[11:18]
-        gt_ref, gq_ref, gk_ref, gv_ref, go_ref, s_out = refs[18:24]
-        m_outs = refs[24:27]
-        r = list(refs[27:])
-        take = lambda n: [r.pop(0) for _ in range(n)]
-        held = take(11)
-        m_acc, o_acc, (wq_ref, wk_ref, wv_ref, t_ref, gmid_ref) = held[0:3], held[3:6], held[6:11]
-        m_got, o_got = take(3), take(3)
-        sendbuf, got1, got2, acc2, got3 = take(3), take(3), take(3), take(3), take(3)
-        s_acc, s_got, g_ref, part, got_part, loc, send, recv = take(8)
-        c = coords()
-        loads = [pltpu.make_async_copy(a, b, loc.at[i]) for i, (a, b) in enumerate(zip(late, held))]
-        for copy in loads:
-            copy.start()
-        core = lax.axis_index("tensor")
-        barrier(core=True)
-        sems = iter(range(256))
-
-        def push(src, dst, device):
-            n = next(sems)
-            copy = remote(src, dst, send.at[n], recv.at[n], device)
-            copy.start()
-            return copy
-
-        def share(acc, got, axis):
-            copies = []
-            for k in (1, 2, 3):
-                rows = pl.ds(pl.multiple_of(((c[axis] + k) % 4) * 24, 8), 24)
-                copies.append(push(acc.at[rows, :], got.at[k - 1], peer(axis, k)))
-            return copies
 
         cos_t, sin_t = cos_ref[...], sin_ref[...]
         for qb in range(8):
@@ -769,32 +741,48 @@
             cs, sn = cos_t[rows], sin_t[rows]
             for h in range(6):
                 v = dq[h * Q_BLK : (h + 1) * Q_BLK]
-                g_ref[rows, h * 128 : (h + 1) * 128] = (v * cs - swap_halves(v) * sn).astype(BF16)
-        dk = jnp.concatenate([dkv_ref[0:64, :], dkv_ref[128:192, :]], axis=0)
-        g_ref[:, 768:896] = (dk * cos_t - swap_halves(dk) * sin_t).astype(BF16)
-        g_ref[:, 896:] = jnp.concatenate([dkv_ref[64:128, :], dkv_ref[192:256, :]], axis=0).astype(BF16)
-
-        pending = [[], [], []]
-        for p, (lo, hi, order) in enumerate(QKV_PARTS):
-            slab_products(sendbuf[p], nt_ref, g_ref[:, lo:hi], order)
-            for k in (1, 2, 3):
-                there = (c[order[0]] + k) % 4
-                pending[p].append(push(sendbuf[p].at[there], got1[p].at[k - 1], peer(order[0], k)))
-
-        for copy in loads:
+                gp_ref[rows, h * 128 : (h + 1) * 128] = (v * cs - swap_halves(v) * sn).astype(BF16)
+        for p in range(3):
+            qkv_first(p)
+        kv_stage(0, 1)
+        m_copies = [None] * 3
+        for m in (0, 2, 1):
+            second_axis_sum(m)
+            m_copies[m] = share(acc2[m], m_got[m], MLP_AXES[m][0])
+        w_ref = [sendbuf[0].at[:, :, h * 128 : (h + 1) * 128] for h in range(8)]
+        w_from = [w_hbm[0].at[h] for h in range(6)] + [w_hbm[1], w_hbm[2]]
+        w_loads = [pltpu.make_async_copy(w_from[h], w_ref[h], loc.at[7 + n_late + h]) for h in range(8)]
+        for copy in w_loads:
+            copy.start()
+
+        def back_through(lo, hi):
+            total = nt(gp_ref[:, lo * 128 : (lo + 1) * 128], w_ref[lo][...].reshape(1536, 128))
+            for h in range(lo + 1, hi):
+                total = total + nt(gp_ref[:, h * 128 : (h + 1) * 128], w_ref[h][...].reshape(1536, 128))
+            return total
+
+        for p in range(3):
+            out_second(p)
+        kv_stage(0, 2)
+        for copy in loads[7:] + w_loads:
             copy.wait()
-        o_copies = [share(o_acc[p], o_got[p], OUT_ORDERS[p][2]) for p in range(3)]
-        m_copies = [share(m_acc[m], m_got[m], MLP_AXES[m][0]) for m in range(3)]
-        total = nt(g_ref[:, 768:896], wk_ref[...]) + nt(g_ref[:, 896:], wv_ref[...])
-        for h in range(6):
-            total = total + nt(g_ref[:, h * 128 : (h + 1) * 128], wq_ref[h])
-        part[...] = total
+        part[...] = back_through(0, 6)
+        kv_stage(1, 3)
+        kv_stage(0, 3)
+
+        dk = jnp.concatenate([own_ref[0:64, :], own_ref[128:192, :]], axis=0)
+        gp_ref[:, 768:896] = (dk * cos_t - swap_halves(dk) * sin_t).astype(BF16)
+        gp_ref[:, 896:] = jnp.concatenate([own_ref[64:128, :], own_ref[192:256, :]], axis=0).astype(BF16)
+        qkv_first(3)
+        qkv_first(4)
+        part[...] += back_through(6, 8)
         swap = push(part, got_part, partner())
 
         inputs = t_ref[...].astype(F32)
         inv = lax.rsqrt(jnp.mean(inputs * inputs, axis=1, keepdims=True) + 1e-06)
         d_norm1 = jnp.sum(part[...] * inputs * inv, axis=0, keepdims=True)
-        d_bias = jnp.sum(g_ref[...].astype(F32), axis=0, keepdims=True)
+        d_bias = jnp.sum(gp_ref[...].astype(F32), axis=0, keepdims=True)
+        core = lax.axis_index("tensor")
         for j in range(12):
             s_acc[0, j : j + 1, :] = d_norm1[:, j * 128 : (j + 1) * 128]
             s_acc[0, 12 + j : 13 + j, :] = dn2_ref[:, j * 128 : (j + 1) * 128]
@@ -827,75 +815,73 @@
 
         send_small(0)
         for p in range(3):
+            qkv_second(p)
+        o_copies = [None] * 3
+        for p in range(3):
+            out_sum(p)
+            o_copies[p] = share(o_acc2[p], o_got[p], OUT_ORDERS[p][2])
+        s_acc[1] = sum_small(0)
+        send_small(1)
+        qkv_second(3)
+        qkv_second(4)
+        swap.wait()
+        g_norm = part[...] + got_part[...]
+        scaled = g_norm * gain_ref[0:1, :]
+        gt_ref[...] += (
+            inv * scaled - inputs * (inv * inv * inv) * jnp.mean(scaled * inputs, axis=1, keepdims=True)
+        )
+        for p in range(3):
+            qkv_third(p)
+        s_acc[2] = sum_small(1)
+        send_small(2)
+        qkv_third(3)
+        qkv_third(4)
+        for p in range(3):
             for copy in o_copies[p]:
                 copy.wait()
             rows = pl.ds(pl.multiple_of(c[OUT_ORDERS[p][2]] * 24, 8), 24)
-            total = o_acc[p][rows, :]
+            total = o_acc2[p][rows, :]
             for k in range(3):
                 total = total + o_got[p][k]
             for j in range(2):
                 go_ref[p * 2 + j] = total[:, j * 128 : (j + 1) * 128]
-        s_acc[1] = sum_small(0)
-        send_small(1)
-        swap.wait()
-        g_norm = part[...] + got_part[...]
-        scaled = g_norm * gain_ref[0:1, :]
-        gt_ref[...] = gmid_ref[...] + (
-            inv * scaled - inputs * (inv * inv * inv) * jnp.mean(scaled * inputs, axis=1, keepdims=True)
-        )
-        for p, (lo, hi, order) in enumerate(QKV_PARTS):
-            own = c[order[0]]
-            sum_first(sendbuf[p], got1[p], pending[p], own)
-            pending[p] = []
-            for k in (1, 2, 3):
-                rows = pl.ds(pl.multiple_of(((c[order[1]] + k) % 4) * 96, 32), 96)
-                pending[p].append(push(sendbuf[p].at[own, rows, :], got2[p].at[k - 1], peer(order[1], k)))
-        s_acc[2] = sum_small(1)
-        send_small(2)
         for m in range(3):
             for copy in m_copies[m]:
                 copy.wait()
             here = c[MLP_AXES[m][0]]
-            m_outs[m][:, pl.ds(col_start(here), FC)] = m_acc[m][pl.ds(pl.multiple_of(here * 24, 8), 24), :]
+            m_outs[m][:, pl.ds(col_start(here), FC)] = acc2[m][pl.ds(pl.multiple_of(here * 24, 8), 24), :]
             for k in (1, 2, 3):
                 m_outs[m][:, pl.ds(col_start((here + 4 - k) % 4), FC)] = m_got[m][k - 1]
-        for p, (lo, hi, order) in enumerate(QKV_PARTS):
-            for copy in pending[p]:
-                copy.wait()
-            own = c[order[0]]
-            rows = pl.ds(pl.multiple_of(c[order[1]] * 96, 32), 96)
-            total = sendbuf[p][own, rows, :].astype(F32)
-            for k in range(3):
-                total = total + got2[p][k].astype(F32)
-            acc2[p][...] = total
-            pending[p] = share(acc2[p], got3[p], order[2])
         s_acc[3] = sum_small(2)
         send_small(3)
-        for p, (lo, hi, order) in enumerate(QKV_PARTS):
-            for copy in pending[p]:
-                copy.wait()
-            rows = pl.ds(pl.multiple_of(c[order[2]] * 24, 8), 24)
-            total = acc2[p][rows, :]
-            for k in range(3):
-                total = total + got3[p][k]
-            for j in range(lo // 128, hi // 128):
-                v = total[:, j * 128 - lo : (j + 1) * 128 - lo]
-                if j < 6:
-                    gq_ref[j] = v
-                elif j == 6:
-                    gk_ref[...] = v
-                else:
-                    gv_ref[...] = v
+        for p in range(n_parts):
+            qkv_out(p)
         s_out[...] = sum_small(3)
 
+    rows = [rn for _, rn, _ in KV_CHUNK] * 2
     cols = [hi - lo for lo, hi, _ in QKV_PARTS]
-    late = (*mlp_acc, *out_acc, wq, wk, wv, tokens, g_mid)
+    late = (tokens, g_mid)
     scratch = (
-        [pltpu.VMEM(v.shape, v.dtype) for v in late]
+        [pltpu.VMEM((4, 384, 512), BF16)] * 3
+        + [pltpu.VMEM((512, FC), BF16)] * 3
+        + [pltpu.VMEM((4, 4, 4, 256, 128), BF16)]
+        + [pltpu.VMEM((128, 1536), BF16)]
+        + [pltpu.VMEM((96, FC), F32)] * 3
+        + [pltpu.VMEM((96, 256), F32)] * 3
+        + [pltpu.VMEM((8, 128, 96), F32), pltpu.VMEM((256, 128), F32)]
+        + [pltpu.VMEM((4, 384, FC), BF16)] * 3
+        + [pltpu.VMEM((2, 192, FC), BF16)] * 3
+        + [pltpu.VMEM((2, 192, FC), BF16)] * 3
+        + [pltpu.VMEM((2, 192, FC), BF16)] * 3
+        + [pltpu.VMEM((3, 96, FC), BF16)] * 3
+        + [pltpu.VMEM((4, 384, 256), BF16)]
+        + [pltpu.VMEM((3, 384, 256), BF16)] * 3
+        + [pltpu.VMEM((3, 96, 256), BF16)] * 3
+        + [pltpu.VMEM((3, 4, 4, r, 128), BF16) for r in rows]
+        + [pltpu.VMEM((3, 4, r, 128), BF16) for r in rows]
+        + [pltpu.VMEM((3, r, 128), BF16) for r in rows]
         + [pltpu.VMEM((3, 24, FC), F32)] * 3
         + [pltpu.VMEM((3, 24, 256), F32)] * 3
-        + [pltpu.VMEM((4, 384, n), BF16) for n in cols]
-        + [pltpu.VMEM((3, 384, n), BF16) for n in cols]
         + [pltpu.VMEM((3, 96, n), BF16) for n in cols]
         + [pltpu.VMEM((96, n), F32) for n in cols]
         + [pltpu.VMEM((3, 24, n), F32) for n in cols]
@@ -905,35 +891,39 @@
             pltpu.VMEM((128, 1024), BF16),
             pltpu.VMEM((128, 1536), F32),
             pltpu.VMEM((128, 1536), F32),
-            DMA((11,)),
-            DMA((64,)),
-            DMA((64,)),
+            DMA((7 + n_late + 8,)),
+            DMA((192,)),
+            DMA((192,)),
         ]
     )
+    vm, sm, hbm = (pl.BlockSpec(memory_space=m) for m in (pltpu.VMEM, pltpu.SMEM, pl.ANY))
     f32 = lambda *s: jax.ShapeDtypeStruct(s, F32)
     shape = (f32(128, 1536), f32(6, 24, 128), f32(24, 128), f32(24, 128), f32(6, 24, 128), f32(SMALL, 128))
     shape = shape + (f32(24, 4480),) * 3
-    vm, hbm = pl.BlockSpec(memory_space=pltpu.VMEM), pl.BlockSpec(memory_space=pl.ANY)
     return pl.pallas_call(
         body,
         out_shape=shape,
-        in_specs=[hbm] * 11 + [vm] * 7,
+        in_specs=[sm] + [hbm] * (10 + n_late) + [vm] * 11,
         out_specs=(vm,) * 9,
         scratch_shapes=scratch,
-        compiler_params=pltpu.CompilerParams(collective_id=3, has_side_effects=True, vmem_limit_bytes=VMEM_BYTES),
-        name="finish",
-    )(*late, dq_t, dkv, cos, sin, norm_t, gain, d_norm2)
+        compiler_params=pltpu.CompilerParams(collective_id=2, has_side_effects=True, vmem_limit_bytes=VMEM_BYTES),
+        name="backward",
+    )(lengths, *xs_in, *gs_in, kv, wq.reshape(6, 4, 384, 128), wk.reshape(4, 384, 128), wv.reshape(4, 384, 128), *late, q, g, lse, delta, branch_t, attn_low, cos, sin, norm_t, gain, d_norm2)
 
 
 def hand_out(*arrays):
     n = len(arrays)
 
     def body(*refs):
-        ins, outs, sem = refs[:n], refs[n : 2 * n], refs[2 * n]
-        copies = [pltpu.make_async_copy(a, b, sem.at[i]) for i, (a, b) in enumerate(zip(ins, outs))]
-        for copy in copies:
+        ins, outs, held, sem = refs[:n], refs[n : 2 * n], refs[2 * n : 3 * n], refs[3 * n]
+        to = [pltpu.make_async_copy(a, b, sem.at[i]) for i, (a, b) in enumerate(zip(ins, held))]
+        back = [pltpu.make_async_copy(a, b, sem.at[n + i]) for i, (a, b) in enumerate(zip(held, outs))]
+        for copy in to:
             copy.start()
-        for copy in copies:
+        for i in range(n):
+            to[i].wait()
+            back[i].start()
+        for copy in back:
             copy.wait()
 
     hbm = pl.BlockSpec(memory_space=pl.ANY)
@@ -942,7 +932,8 @@
         out_shape=tuple(jax.ShapeDtypeStruct(v.shape, v.dtype) for v in arrays),
         in_specs=[hbm] * n,
         out_specs=(hbm,) * n,
-        scratch_shapes=[DMA((n,))],
+        scratch_shapes=[pltpu.VMEM(v.shape, v.dtype) for v in arrays] + [DMA((2 * n,))],
+        compiler_params=pltpu.CompilerParams(vmem_limit_bytes=VMEM_BYTES),
         name="hand_out",
     )(*arrays)
 
@@ -964,9 +955,9 @@
     output, g_mid, branch_t, g_attn, delta, d_norm2, *shared = feed_forward(
         branch, attn, tokens, cotangent, gains, wo, w_gate, w_up, w_down
     )
-    *acc, dq_t, dkv = backward(shared[:3], shared[3:], q, g_attn, kv, lse, delta, branch_t, attn_low, lengths)
-    grad_tokens, grad_wq, grad_wk, grad_wv, grad_wo, sums, grad_gate, grad_up, grad_down = finish(
-        acc[:3], acc[3:], dq_t, dkv, cos, sin, norm_t, wq, wk, wv, tokens, gains, g_mid, d_norm2
+    grad_tokens, grad_wq, grad_wk, grad_wv, grad_wo, sums, grad_gate, grad_up, grad_down = backward(
+        shared[:3], shared[3:], q, g_attn, kv.reshape(4, 4, 4, 256, 128), lse, delta, branch_t, attn_low, lengths,
+        cos, sin, norm_t, wq, wk, wv, tokens, gains, g_mid, d_norm2,
     )
     output, grad_tokens, grad_wq, grad_wk, grad_wv, grad_wo, grad_gate, grad_up, grad_down = hand_out(
         output, grad_tokens, grad_wq, grad_wk, grad_wv, grad_wo, grad_gate, grad_up, grad_down

time: 328 us -> 223 us (0.68)
  Pallas kernels: 319 us -> 213 us
    pallas_call x1, Pallas kernels: 93.1 us -> 2.91 us  [hand_out(): pl.pallas_call(body, out_shape=tuple((jax.ShapeDtypeStruct(v.shape, v.dty...]
    pallas_call x2 -> x1, Pallas kernels: 130 us -> 115 us  [backward(): pl.pallas_call(body, out_shape=shape, in_specs=[sm] + [hbm] * (10 + n_lat...]
where the time goes in v1:
time: 223 us; the launch traced here: 219 us
  Pallas kernels  213 us (96%)
  local copies, waits for them, and re-layouts  4.69 us (2%)
    pallas_call x1, Pallas kernels, backward(): pl.pallas_call(body, out_shape=shape, in_specs=[sm] + [hbm] * (10 + n_lat...  115 us
    pallas_call x1, Pallas kernels, feed_forward(): pl.pallas_call(body, out_shape=(f32(128, 1536), f32(128, 1536), b16(1536,...  41 us
    pallas_call x1, Pallas kernels, qkv_gather(): pl.pallas_call(body, out_shape=(jax.ShapeDtypeStruct((8, 96, 128), BF16),...  37.8 us
    pallas_call x1, Pallas kernels, attn_forward(): pl.pallas_call(body, out_shape=(jax.ShapeDtypeStruct((128, 1536), F32), j...  16.3 us

profile of v1, /device:TPU:0, one launch (start us, length us, event | category | flops | bytes accessed | tf_op | source)
XLA Modules:
  0.0 219.1 jit_solution(1647987388660724149)
XLA Ops:
  0.6 0.7 stack.10
  1.3 0.7 stack.9
  2.0 0.6 pad_maximum_fusion.g_ref.refs_22_
  2.7 37.8 %qkv_gather.1 = (bf16[8,96,128]{2,1,0:T(8,128)(2,1)}, bf16[4,4,4,256,128]{4,3,2,1,0:T(8,128)(2,1)}, bf16[1536,128]{1,0:T(8,128)(2,1)}, f32[128,128]{1,0:T(8,128)}, f32[128,128]{1,0:T(8,128)}) custom-call(s32[8]{0:T(128)} %refs_0_.1, bf16[128,1536]{1,0:T(8,128)(2,1)} %refs_11_.1, f32[2,1536]{1,0:T(2,128)} %pad_maximum_fusion.g_ref.refs_22_, ...), custom_call_target="tpu_custom_call" | custom-call | tf_op jit(solution)/shard_map/qkv_gather/pallas_call | solution.py:127
  40.5 16.3 %attn_forward.1 = (f32[128,1536]{1,0:T(8,128)}, f32[8,96,128]{2,1,0:T(8,128)}, bf16[128,768]{1,0:T(8,128)(2,1)}, f32[8,1,96]{2,1,0:T(1,128)}) custom-call(s32[8]{0:T(128)} %refs_0_.1, bf16[8,96,128]{2,1,0:T(8,128)(2,1)} %get-tuple-element.53.q_ref.refs_13_, bf16[64,256,128]{2,1,0:T(8,128)(2,1)} %bitcast.20, bf16[768,1536]{1,0:T(8,128)(2,1)} %bitcast.21), custom_call_target="tpu_custom_call" | custom-call | tf_op jit(solution)/shard_map/attn_forward/pallas_call | solution.py:221
  56.8 41.0 %feed_forward.1 = (f32[128,1536]{1,0:T(8,128)}, f32[128,1536]{1,0:T(8,128)}, bf16[1536,128]{1,0:T(8,128)(2,1)}, bf16[8,96,128]{2,1,0:T(8,128)(2,1)}, f32[8,1,96]...) custom-call(f32[128,1536]{1,0:T(8,128)} %get-tuple-element.55.br_ref, ...), custom_call_target="tpu_custom_call" | custom-call | tf_op jit(solution)/shard_map/feed_forward/pallas_call | solution.py:403
  97.8 114.9 %backward.1 = (f32[128,1536]{1,0:T(8,128)}, f32[6,24,128]{2,1,0:T(8,128)}, f32[24,128]{1,0:T(8,128)}, f32[24,128]{1,0:T(8,128)}, f32[6,24,128]{2,1,0:T(8,128)}, ...) custom-call(s32[8]{0:T(128)} %refs_0_.1, ...), custom_call_target="tpu_custom_call" | custom-call | tf_op jit(solution)/shard_map/backward/pallas_call | solution.py:903
  212.7 2.9 %hand_out.1 = (f32[128,1536]{1,0:T(8,128)}, f32[128,1536]{1,0:T(8,128)}, f32[6,24,128]{2,1,0:T(8,128)}, f32[24,128]{1,0:T(8,128)}, f32[24,128]{1,0:T(8,128)}, /*...) custom-call(f32[128,1536]{1,0:T(8,128)} %get-tuple-element.57.refs_0_, ...), custom_call_target="tpu_custom_call" | custom-call | tf_op jit(solution)/shard_map/hand_out/pallas_call | solution.py:930
  215.6 1.4 fusion
  217.0 0.7 dynamic_slice.10
  217.7 0.7 copy.29
  218.4 0.5 fusion.1

commit v2 on v1

--- a/solution.py
+++ b/solution.py
@@ -78,69 +78,6 @@
     return pltpu.roll(v, 64, 1)
 
 
-def qkv_gather(tokens, gain, wq, wk, wv, bq, bk, bv, lengths):
-    def body(len_ref, t_ref, g_ref, wq_ref, wk_ref, wv_ref, bq_ref, bk_ref, bv_ref,
-             q_out, out, nt_out, cos_out, sin_out, wq_buf, loc, send, recv):
-        c = coords()
-        load = pltpu.make_async_copy(wq_ref, wq_buf, loc)
-        load.start()
-        x = t_ref[...].astype(F32)
-        inv = lax.rsqrt(jnp.mean(x * x, axis=1, keepdims=True) + 1e-06)
-        normed = (x * inv * g_ref[0:1, :]).astype(BF16)
-        cos, sin = rope_tables(len_ref)
-        cos_out[...], sin_out[...] = cos, sin
-        k_pre = jnp.dot(normed, wk_ref[...], preferred_element_type=F32) + bk_ref[...].astype(F32)
-        v_pre = jnp.dot(normed, wv_ref[...], preferred_element_type=F32) + bv_ref[...].astype(F32)
-        k_rot = (k_pre * cos + swap_halves(k_pre) * sin).astype(BF16)
-        v_low = v_pre.astype(BF16)
-        out[c["z"], c["x"], c["y"]] = jnp.concatenate([k_rot[:64], v_low[:64], k_rot[64:], v_low[64:]], axis=0)
-        barrier()
-        parts = [(r0 + 128 * chunk, rn, order) for chunk in range(2) for r0, rn, order in KV_CHUNK]
-        pending = [[] for _ in parts]
-
-        def send_stage(stage):
-            for p, (r0, rn, order) in enumerate(parts):
-                for copy in pending[p]:
-                    copy.wait()
-                pending[p] = []
-                idx = kv_index(order[:stage], c, r0, rn)
-                for k in (1, 2, 3):
-                    n = (p * 3 + stage) * 3 + k - 1
-                    copy = remote(out.at[idx], out.at[idx], send.at[n], recv.at[n], peer(order[stage], k))
-                    copy.start()
-                    pending[p].append(copy)
-
-        send_stage(0)
-        load.wait()
-        for h in range(6):
-            q = jnp.dot(normed, wq_buf[h], preferred_element_type=F32) + bq_ref[h : h + 1, :].astype(F32)
-            q = (q * cos + swap_halves(q) * sin).astype(BF16)
-            q_out[:, h * Q_BLK : (h + 1) * Q_BLK, :] = q.reshape(8, Q_BLK, 128)
-        send_stage(1)
-        nt_out[...] = normed.T
-        send_stage(2)
-        for copies in pending:
-            for copy in copies:
-                copy.wait()
-
-    vm, sm = pl.BlockSpec(memory_space=pltpu.VMEM), pl.BlockSpec(memory_space=pltpu.SMEM)
-    return pl.pallas_call(
-        body,
-        out_shape=(
-            jax.ShapeDtypeStruct((8, 96, 128), BF16),
-            jax.ShapeDtypeStruct((4, 4, 4, 256, 128), BF16),
-            jax.ShapeDtypeStruct((1536, 128), BF16),
-            jax.ShapeDtypeStruct((128, 128), F32),
-            jax.ShapeDtypeStruct((128, 128), F32),
-        ),
-        in_specs=[sm, vm, vm, pl.BlockSpec(memory_space=pl.ANY)] + [vm] * 5,
-        out_specs=(vm,) * 5,
-        scratch_shapes=[pltpu.VMEM((6, 1536, 128), BF16), DMA, DMA((54,)), DMA((54,))],
-        compiler_params=pltpu.CompilerParams(collective_id=0, has_side_effects=True, vmem_limit_bytes=VMEM_BYTES),
-        name="qkv_gather",
-    )(lengths, tokens, gain, wq, wk, wv, bq, bk, bv)
-
-
 Q_BLK = 16
 BLK = Q_BLK * 64
 SCALE = 1.0 / math.sqrt(128)
@@ -154,84 +91,6 @@
         end = end + len_ref[j]
         start = jnp.where(pos >= end, end, start)
     return start
-
-
-def doc_start_scalar(pos, len_ref):
-    start, end = jnp.int32(0), jnp.int32(0)
-    for j in range(8):
-        end = end + len_ref[j]
-        start = jnp.where(pos >= end, end, start)
-    return start
-
-
-def attn_forward(q, kv, w_out, lengths):
-    def body(len_ref, q_ref, kv_hbm, wo_hbm, part_ref, out_ref, low_ref, lse_ref, kv_ref, wo_ref, loc):
-        loads = [
-            pltpu.make_async_copy(kv_hbm.at[:, pl.ds(0, 128), :], kv_ref.at[:, pl.ds(0, 128), :], loc.at[0]),
-            pltpu.make_async_copy(kv_hbm.at[:, pl.ds(128, 128), :], kv_ref.at[:, pl.ds(128, 128), :], loc.at[1]),
-            pltpu.make_async_copy(wo_hbm, wo_ref, loc.at[2]),
-        ]
-        for copy in loads:
-            copy.start()
-        dev = lax.axis_index("seq")
-        col = lax.broadcasted_iota(jnp.int32, (96, BLK), 1)
-        key_off = (col % Q_BLK) * 64 + col // Q_BLK
-        row_off = (lax.broadcasted_iota(jnp.int32, (96, 1), 0) % Q_BLK) * 64 + dev
-
-        def q_step(qb, _):
-            q_blk = q_ref[qb]
-            pos_q = row_off + qb * BLK
-            start_q = doc_bounds(pos_q, len_ref)
-            lo = doc_start_scalar(qb * BLK + dev, len_ref) // BLK
-
-            def k_step(kb, carry):
-                m, l, acc = carry
-                k_blk = kv_ref[:, kv_rows(kb, 0), :].reshape(BLK, 128)
-                v_blk = kv_ref[:, kv_rows(kb, 1), :].reshape(BLK, 128)
-                s = lax.dot_general(q_blk, k_blk, (((1,), (1,)), ((), ())), preferred_element_type=F32)
-                pos_k = key_off + kb * BLK
-                vis = (pos_k <= pos_q) & (pos_k >= start_q)
-                s = jnp.where(vis, s * SCALE2, -1e30)
-                m_new = jnp.maximum(m, jnp.max(s, axis=1, keepdims=True))
-                p = jnp.where(vis, jnp.exp2(s - m_new), 0.0)
-                a = jnp.exp2(m - m_new)
-                l = l * a + jnp.sum(p, axis=1, keepdims=True)
-                acc = acc * a + jnp.dot(p.astype(BF16), v_blk, preferred_element_type=F32)
-                return m_new, l, acc
-
-            init = (jnp.full((96, 1), -1e30, F32), jnp.zeros((96, 1), F32), jnp.zeros((96, 128), F32))
-            m, l, acc = lax.fori_loop(lo, qb + 1, k_step, init)
-            attn = acc / l
-            out_ref[qb] = attn
-            low = attn.astype(BF16)
-            for h in range(6):
-                rows = pl.ds(pl.multiple_of(qb * Q_BLK, Q_BLK), Q_BLK)
-                low_ref[rows, h * 128 : (h + 1) * 128] = low[h * Q_BLK : (h + 1) * Q_BLK]
-            lse_ref[qb] = jnp.broadcast_to(m + jnp.log2(l), (96, 128)).T[0:1]
-            return 0
-
-        loads[0].wait()
-        lax.fori_loop(0, 4, q_step, 0)
-        loads[1].wait()
-        lax.fori_loop(4, 8, q_step, 0)
-        loads[2].wait()
-        part_ref[...] = jnp.dot(low_ref[...], wo_ref[...], preferred_element_type=F32)
-
-    vm = pl.BlockSpec(memory_space=pltpu.VMEM)
-    return pl.pallas_call(
-        body,
-        out_shape=(
-            jax.ShapeDtypeStruct((128, 1536), F32),
-            jax.ShapeDtypeStruct((8, 96, 128), F32),
-            jax.ShapeDtypeStruct((128, 768), BF16),
-            jax.ShapeDtypeStruct((8, 1, 96), F32),
-        ),
-        in_specs=[pl.BlockSpec(memory_space=pltpu.SMEM), vm] + [pl.BlockSpec(memory_space=pl.ANY)] * 2,
-        out_specs=(vm,) * 4,
-        scratch_shapes=[pltpu.VMEM((64, 256, 128), BF16), pltpu.VMEM((768, 1536), BF16), DMA((3,))],
-        compiler_params=pltpu.CompilerParams(vmem_limit_bytes=VMEM_BYTES),
-        name="attn_forward",
-    )(lengths, q, kv, w_out)
 
 
 FC = 1152
@@ -263,14 +122,17 @@
     return jnp.concatenate(rows, axis=0)
 
 
-def feed_forward(branch, attn, tokens, cot, gain, w_out, w_gate, w_up, w_down):
-    def body(br_ref, at_ref, t_ref, c_ref, g_ref, wo_hbm, wg_hbm, wu_hbm, wd_hbm,
-             out_ref, gmid_ref, bt_ref, ga_ref, delta_ref, dn_ref, x0, x1, x2, g0, g1, g2,
+def forward(tokens, cot, lengths, gains, wq, wk, wv, bq, bk, bv, w_out, w_gate, w_up, w_down):
+    def body(len_ref, t_ref, c_ref, g_ref, wk_ref, wv_ref, bq_ref, bk_ref, bv_ref, wq_hbm, wo_hbm, wg_hbm, wu_hbm, wd_hbm,
+             out_ref, gmid_ref, bt_ref, ga_ref, delta_ref, dn_ref, q_ref, nt1_ref, cos_out, sin_out, low_ref, lse_ref,
+             x0, x1, x2, g0, g1, g2, kv_hbm,
+             kv, wq_ref, at_ref, m_ref, l_ref, acc_ref, br_ref,
              wo_ref, wg, wu, wd, got_br, acc, got, mid_ref, norm_ref, nt_ref, ct_ref, act, w_sem, loc, send, recv):
         xs, gs = (x0, x1, x2), (g0, g1, g2)
         c = coords()
+        dev = lax.axis_index("seq")
         turn = c["z"] + c["x"] + c["y"]
-        sems = iter(range(64))
+        sems = iter(range(128))
 
         def load(j):
             cols = pl.ds(col_start((turn + j) % 4), FC)
@@ -284,24 +146,129 @@
                 copy.start()
             return copies
 
-        loads = [load(0), load(1)]
-        barrier(core=True)
-
         def push(src, dst, device):
             n = next(sems)
             copy = remote(src, dst, send.at[n], recv.at[n], device)
             copy.start()
             return copy
 
-        later = []
-        ex = push(br_ref, got_br, partner())
+        def keep(src, dst, n):
+            copy = pltpu.make_async_copy(src, dst, loc.at[n])
+            copy.start()
+            return copy
+
+        wq_load = keep(wq_hbm, wq_ref, 6)
+        wo_load = keep(wo_hbm, wo_ref, 7)
+
+        x = t_ref[...].astype(F32)
+        inv = lax.rsqrt(jnp.mean(x * x, axis=1, keepdims=True) + 1e-06)
+        normed = (x * inv * g_ref[0:1, :]).astype(BF16)
+        cos, sin = rope_tables(len_ref)
+        cos_out[...], sin_out[...] = cos, sin
+        k_pre = mm(normed, wk_ref[...]) + bk_ref[...].astype(F32)
+        v_low = (mm(normed, wv_ref[...]) + bv_ref[...].astype(F32)).astype(BF16)
+        k_rot = (k_pre * cos + swap_halves(k_pre) * sin).astype(BF16)
+        kv[c["z"], c["x"], c["y"]] = jnp.concatenate([k_rot[:64], v_low[:64], k_rot[64:], v_low[64:]], axis=0)
+        barrier(core=True)
+        kv_pending = [[] for _ in range(6)]
+
+        def kv_wait(chunk):
+            for p in range(chunk * 3, chunk * 3 + 3):
+                for copy in kv_pending[p]:
+                    copy.wait()
+                kv_pending[p] = []
+
+        def kv_stage(chunk, stage):
+            for i, (r0, rn, order) in enumerate(KV_CHUNK):
+                p, r0 = chunk * 3 + i, r0 + chunk * 128
+                for copy in kv_pending[p]:
+                    copy.wait()
+                idx = kv_index(order[:stage], c, r0, rn)
+                kv_pending[p] = [push(kv.at[idx], kv.at[idx], peer(order[stage], k)) for k in (1, 2, 3)]
+
+        kv_stage(0, 0)
+        kv_stage(1, 0)
+        wq_load.wait()
+        for h in range(6):
+            q = mm(normed, wq_ref[h]) + bq_ref[h : h + 1, :].astype(F32)
+            q = (q * cos + swap_halves(q) * sin).astype(BF16)
+            q_ref[:, h * Q_BLK : (h + 1) * Q_BLK, :] = q.reshape(8, Q_BLK, 128)
+        kv_stage(0, 1)
+        kv_stage(1, 1)
+        nt1_ref[...] = normed.T
+        kv_stage(0, 2)
+        loads = [load(0), load(1)]
         ct_ref[...] = c_ref[...].T.reshape(4, 384, 128)
-        own = [pltpu.make_async_copy(ct_ref, x2.at[:, :, pl.ds(0, 128)], loc.at[3])]
-        own[0].start()
-        for k in (1, 2, 3):
-            later.append(push(ct_ref, x2.at[:, :, pl.ds(k * 128, 128)], peer("y", k)))
-        ex.wait()
-        mid = t_ref[...].astype(F32) + (br_ref[...] + got_br[...])
+        own = [keep(ct_ref, x2.at[:, :, pl.ds(0, 128)], 3)]
+        kv_wait(0)
+        kv_stage(1, 2)
+        later = [push(ct_ref, x2.at[:, :, pl.ds(k * 128, 128)], peer("y", k)) for k in (1, 2, 3)]
+
+        row_off = (lax.broadcasted_iota(jnp.int32, (96, 1), 0) % Q_BLK) * 64 + dev
+        col = lax.broadcasted_iota(jnp.int32, (96, BLK), 1)
+        key_off = (col % Q_BLK) * 64 + col // Q_BLK
+
+        def attend(qb, lo, hi, carry, diagonal):
+            q_blk = q_ref[qb]
+            pos_q = row_off + qb * BLK
+            start_q = doc_bounds(pos_q, len_ref)
+
+            def block(kb, carry, causal):
+                m, l, acc = carry
+                k_blk = kv[:, :, :, kv_rows(kb, 0), :].reshape(BLK, 128)
+                v_blk = kv[:, :, :, kv_rows(kb, 1), :].reshape(BLK, 128)
+                pos_k = key_off + kb * BLK
+                vis = pos_k >= start_q
+                if causal:
+                    vis = vis & (pos_k <= pos_q)
+                s = jnp.where(vis, nt(q_blk, k_blk) * SCALE2, -1e30)
+                m_new = jnp.maximum(m, jnp.max(s, axis=1, keepdims=True))
+                p = jnp.exp2(s - m_new)
+                a = jnp.exp2(m - m_new)
+                return m_new, l * a + jnp.sum(p, axis=1, keepdims=True), acc * a + mm(p.astype(BF16), v_blk)
+
+            carry = lax.fori_loop(lo, hi, lambda kb, carry: block(kb, carry, False), carry)
+            return block(qb, carry, True) if diagonal else carry
+
+        def attend_end(qb, carry):
+            m, l, acc = carry
+            attn = acc / l
+            at_ref[qb] = attn
+            low = attn.astype(BF16)
+            for h in range(6):
+                rows = pl.ds(pl.multiple_of(qb * Q_BLK, Q_BLK), Q_BLK)
+                low_ref[rows, h * 128 : (h + 1) * 128] = low[h * Q_BLK : (h + 1) * Q_BLK]
+            lse_ref[qb] = jnp.broadcast_to(m + jnp.log2(l), (96, 128)).T[0:1]
+
+        init = (jnp.full((96, 1), -1e30, F32), jnp.zeros((96, 1), F32), jnp.zeros((96, 128), F32))
+
+        def upper(qb, _):
+            m_ref[qb - 4], l_ref[qb - 4], acc_ref[qb - 4] = attend(qb, 0, 4, init, False)
+            return 0
+
+        def whole(qb, _):
+            attend_end(qb, attend(qb, 0, qb, init, True))
+            return 0
+
+        def rest(qb, _):
+            attend_end(qb, attend(qb, 4, qb, (m_ref[qb - 4], l_ref[qb - 4], acc_ref[qb - 4]), True))
+            return 0
+
+        out_kv = [keep(kv.at[:, :, :, pl.ds(0, 128), :], kv_hbm.at[:, :, :, pl.ds(0, 128), :], 8)]
+        lax.fori_loop(0, 4, whole, 0)
+        lax.fori_loop(4, 8, upper, 0)
+        kv_wait(1)
+        out_kv.append(keep(kv.at[:, :, :, pl.ds(128, 128), :], kv_hbm.at[:, :, :, pl.ds(128, 128), :], 9))
+        lax.fori_loop(4, 8, rest, 0)
+        wo_load.wait()
+        ex = []
+        for half in range(2):
+            cols = slice(half * 768, (half + 1) * 768)
+            br_ref[half] = mm(low_ref[...], wo_ref[:, cols])
+            ex.append(push(br_ref.at[half], got_br.at[half], partner()))
+        for copy in ex:
+            copy.wait()
+        mid = t_ref[...].astype(F32) + jnp.concatenate([br_ref[h] + got_br[h] for h in range(2)], axis=1)
         mid_ref[...] = mid
         inv = lax.rsqrt(jnp.mean(mid * mid, axis=1, keepdims=True) + 1e-06)
         normed = (mid * inv * g_ref[1:2, :]).astype(BF16)
@@ -309,11 +276,8 @@
         turned = normed.astype(F32).T
         for m in range(2):
             nt_ref[m] = in_order(turned, MLP_AXES[m][1:] + MLP_AXES[m][:1]).astype(BF16).reshape(4, 384, 128)
-        own.append(pltpu.make_async_copy(nt_ref.at[0], x0.at[:, :, pl.ds(0, 128)], loc.at[4]))
-        own.append(pltpu.make_async_copy(nt_ref.at[1], x1.at[:, :, pl.ds(0, 128)], loc.at[5]))
-        own.append(pltpu.make_async_copy(wo_hbm, wo_ref, loc.at[6]))
-        for copy in own[1:]:
-            copy.start()
+        own.append(keep(nt_ref.at[0], x0.at[:, :, pl.ds(0, 128)], 4))
+        own.append(keep(nt_ref.at[1], x1.at[:, :, pl.ds(0, 128)], 5))
         for k in (1, 2, 3):
             for m, w in ((0, "z"), (1, "x")):
                 later.append(push(nt_ref.at[m], xs[m].at[:, :, pl.ds(k * 128, 128)], peer(w, k)))
@@ -339,13 +303,12 @@
             twice = (lane < 128) & (d == 3)
             zero = jnp.zeros((128, FC), BF16)
             hidden, g_gate, g_up = (jnp.where(twice, zero, v) for v in (hidden, g_gate, g_up))
+            add_g = nt(g_gate, wg[b]) + nt(g_up, wu[b])
+            acc[1] = add_g if j == 0 else acc[1] + add_g
+            if j == 3:
+                ex = [push(acc.at[1], got.at[1], partner())]
             add_o = mm(hidden, wd[b])
-            add_g = nt(g_gate, wg[b]) + nt(g_up, wu[b])
-            if j == 0:
-                acc[0], acc[1] = add_o, add_g
-            else:
-                acc[0] += add_o
-                acc[1] += add_g
+            acc[0] = add_o if j == 0 else acc[0] + add_o
             if j + 2 < 4:
                 loads.append(load(j + 2))
             for m in range(3):
@@ -360,11 +323,11 @@
                 @pl.when(k != 0)
                 def _():
                     remote(
-                        act.at[m, j], gs[m].at[slot, :], send.at[32 + m * 4 + j], recv.at[32 + m * 4 + k], peer(w, k)
+                        act.at[m, j], gs[m].at[slot, :], send.at[96 + m * 4 + j], recv.at[96 + m * 4 + k], peer(w, k)
                     ).start()
 
+        ex.append(push(acc.at[0], got.at[0], partner()))
         dn_ref[...] = jnp.sum(acc[1] * mid_ref[...] * inv, axis=0, keepdims=True)
-        ex = [push(acc.at[1], got.at[1], partner()), push(acc.at[0], got.at[0], partner())]
         cot_f = c_ref[...].astype(F32)
         ex[0].wait()
         gn = acc[1] + got[1]
@@ -372,7 +335,6 @@
         scaled = gn * g_ref[1:2, :]
         g_mid = cot_f + (inv * scaled - mid * (inv * inv * inv) * jnp.mean(scaled * mid, axis=1, keepdims=True))
         gmid_ref[...] = g_mid
-        own[3].wait()
         branch_low = g_mid.astype(BF16)
         bt_ref[...] = branch_low.T
         g_attn = nt(branch_low, wo_ref[...]).astype(BF16)
@@ -382,7 +344,7 @@
             delta_ref[qb] = jnp.sum((ga_ref[qb].astype(F32) * at_ref[qb]).T, axis=0, keepdims=True)
         ex[1].wait()
         out_ref[...] = mid_ref[...] + (acc[0] + got[0])
-        for copy in later + own[:3]:
+        for copy in later + own + out_kv:
             copy.wait()
         for m in range(3):
             w = MLP_AXES[m][0]
@@ -394,40 +356,31 @@
                 def _():
                     slot = pl.ds(pl.multiple_of(k * 128, 128), 128)
                     remote(
-                        act.at[m, j], gs[m].at[slot, :], send.at[32 + m * 4 + j], recv.at[32 + m * 4 + k], peer(w, k)
+                        act.at[m, j], gs[m].at[slot, :], send.at[96 + m * 4 + j], recv.at[96 + m * 4 + k], peer(w, k)
                     ).wait()
 
     f32 = lambda *s: jax.ShapeDtypeStruct(s, F32)
     b16 = lambda *s: jax.ShapeDtypeStruct(s, BF16)
-    vm, hbm = pl.BlockSpec(memory_space=pltpu.VMEM), pl.BlockSpec(memory_space=pl.ANY)
+    vm, sm, hbm = (pl.BlockSpec(memory_space=m) for m in (pltpu.VMEM, pltpu.SMEM, pl.ANY))
+    held = [(6, 1536, 128, BF16), (8, 96, 128, F32), (4, 96, 1, F32), (4, 96, 1, F32), (4, 96, 128, F32)]
+    held += [(2, 128, 768, F32), (768, 1536, BF16), (2, 1536, FC, BF16), (2, 1536, FC, BF16), (2, FC, 1536, BF16)]
+    held += [(2, 128, 768, F32), (2, 128, 1536, F32), (2, 128, 1536, F32), (128, 1536, F32), (128, 1536, BF16)]
+    held += [(2, 4, 384, 128, BF16), (4, 384, 128, BF16), (3, 4, 128, FC, BF16)]
     return pl.pallas_call(
         body,
         out_shape=(f32(128, 1536), f32(128, 1536), b16(1536, 128), b16(8, 96, 128), f32(8, 1, 96), f32(1, 1536))
+        + (b16(8, 96, 128), b16(1536, 128), f32(128, 128), f32(128, 128), b16(128, 768), f32(8, 1, 96))
         + (b16(4, 384, 512),) * 3
-        + (b16(512, FC),) * 3,
-        in_specs=[vm] * 5 + [hbm] * 4,
-        out_specs=(vm,) * 6 + (hbm,) * 6,
-        scratch_shapes=[
-            pltpu.VMEM((768, 1536), BF16),
-            pltpu.VMEM((2, 1536, FC), BF16),
-            pltpu.VMEM((2, 1536, FC), BF16),
-            pltpu.VMEM((2, FC, 1536), BF16),
-            pltpu.VMEM((128, 1536), F32),
-            pltpu.VMEM((2, 128, 1536), F32),
-            pltpu.VMEM((2, 128, 1536), F32),
-            pltpu.VMEM((128, 1536), F32),
-            pltpu.VMEM((128, 1536), BF16),
-            pltpu.VMEM((2, 4, 384, 128), BF16),
-            pltpu.VMEM((4, 384, 128), BF16),
-            pltpu.VMEM((3, 4, 128, FC), BF16),
-            DMA((2, 3)),
-            DMA((7,)),
-            DMA((64,)),
-            DMA((64,)),
-        ],
+        + (b16(512, FC),) * 3
+        + (b16(4, 4, 4, 256, 128),),
+        in_specs=[sm] + [vm] * 8 + [hbm] * 5,
+        out_specs=(vm,) * 12 + (hbm,) * 7,
+        scratch_shapes=[pltpu.VMEM((4, 4, 4, 256, 128), BF16)]
+        + [pltpu.VMEM(v[:-1], v[-1]) for v in held]
+        + [DMA((2, 3)), DMA((10,)), DMA((112,)), DMA((112,))],
         compiler_params=pltpu.CompilerParams(collective_id=4, has_side_effects=True, vmem_limit_bytes=VMEM_BYTES),
-        name="feed_forward",
-    )(branch, attn, tokens, cot, gain, w_out, w_gate, w_up, w_down)
+        name="forward",
+    )(lengths, tokens, cot, gains, wk, wv, bq, bk, bv, wq, w_out, w_gate, w_up, w_down)
 
 
 OUT_ORDERS = (("z", "x", "y"), ("x", "y", "z"), ("y", "z", "x"))
@@ -949,14 +902,11 @@
     wo = w_out.reshape(768, 1536)
     gains = jnp.stack([norm1_gain, norm2_gain])
 
-    q, kv, norm_t, cos, sin = qkv_gather(tokens, gains, wq, wk, wv, b_query, b_key, b_value, lengths)
-    kv = kv.reshape(64, 256, 128)
-    branch, attn, attn_low, lse = attn_forward(q, kv, wo, lengths)
-    output, g_mid, branch_t, g_attn, delta, d_norm2, *shared = feed_forward(
-        branch, attn, tokens, cotangent, gains, wo, w_gate, w_up, w_down
+    (output, g_mid, branch_t, g_attn, delta, d_norm2, q, norm_t, cos, sin, attn_low, lse, *shared, kv) = forward(
+        tokens, cotangent, lengths, gains, wq, wk, wv, b_query, b_key, b_value, wo, w_gate, w_up, w_down
     )
     grad_tokens, grad_wq, grad_wk, grad_wv, grad_wo, sums, grad_gate, grad_up, grad_down = backward(
-        shared[:3], shared[3:], q, g_attn, kv.reshape(4, 4, 4, 256, 128), lse, delta, branch_t, attn_low, lengths,
+        shared[:3], shared[3:], q, g_attn, kv, lse, delta, branch_t, attn_low, lengths,
         cos, sin, norm_t, wq, wk, wv, tokens, gains, g_mid, d_norm2,
     )
     output, grad_tokens, grad_wq, grad_wk, grad_wv, grad_wo, grad_gate, grad_up, grad_down = hand_out(

time: 223 us -> 216 us (0.969)
  Pallas kernels: 213 us -> 206 us
    pallas_call x3 -> x1, Pallas kernels: 95.1 us -> 85.4 us  [forward(): pl.pallas_call(body, out_shape=(f32(128, 1536), f32(128, 1536), b16(1536,...]
    pallas_call x1, Pallas kernels: 115 us -> 118 us  [backward(): pl.pallas_call(body, out_shape=shape, in_specs=[sm] + [hbm] * (10 + n_lat...]
where the time goes in v2:
time: 216 us; the launch traced here: 212 us
  Pallas kernels  206 us (95%)
  local copies, waits for them, and re-layouts  4.69 us (2%)
    pallas_call x1, Pallas kernels, backward(): pl.pallas_call(body, out_shape=shape, in_specs=[sm] + [hbm] * (10 + n_lat...  118 us
    pallas_call x1, Pallas kernels, forward(): pl.pallas_call(body, out_shape=(f32(128, 1536), f32(128, 1536), b16(1536,...  85.4 us

profile of v2, /device:TPU:0, one launch (start us, length us, event | category | flops | bytes accessed | tf_op | source)
XLA Modules:
  0.0 212.3 jit_solution(18180258172048422165)
XLA Ops:
  0.6 0.7 stack.10
  1.3 0.7 stack.9
  2.0 0.6 pad_maximum_fusion.g_ref.refs_22_
  2.7 85.4 %forward.1 = (f32[128,1536]{1,0:T(8,128)}, f32[128,1536]{1,0:T(8,128)}, bf16[1536,128]{1,0:T(8,128)(2,1)}, bf16[8,96,128]{2,1,0:T(8,128)(2,1)}, f32[8,1,96]{2,1,...) custom-call(s32[8]{0:T(128)} %refs_0_.1, ...), custom_call_target="tpu_custom_call" | custom-call | tf_op jit(solution)/shard_map/forward/pallas_call | solution.py:369
  88.1 117.8 %backward.1 = (f32[128,1536]{1,0:T(8,128)}, f32[6,24,128]{2,1,0:T(8,128)}, f32[24,128]{1,0:T(8,128)}, f32[24,128]{1,0:T(8,128)}, f32[6,24,128]{2,1,0:T(8,128)}, ...) custom-call(s32[8]{0:T(128)} %refs_0_.1, ...), custom_call_target="tpu_custom_call" | custom-call | tf_op jit(solution)/shard_map/backward/pallas_call | solution.py:856
  205.9 2.9 %hand_out.1 = (f32[128,1536]{1,0:T(8,128)}, f32[128,1536]{1,0:T(8,128)}, f32[6,24,128]{2,1,0:T(8,128)}, f32[24,128]{1,0:T(8,128)}, f32[24,128]{1,0:T(8,128)}, /*...) custom-call(f32[128,1536]{1,0:T(8,128)} %get-tuple-element.51.refs_0_, ...), custom_call_target="tpu_custom_call" | custom-call | tf_op jit(solution)/shard_map/hand_out/pallas_call | solution.py:883
  208.8 1.4 fusion
  210.2 0.7 dynamic_slice.10
  211.0 0.7 copy.29
  211.6 0.5 fusion.1

commit v3 on v2

--- a/solution.py
+++ b/solution.py
@@ -413,6 +413,57 @@
                 buf[y, z * 96 : (z + 1) * 96] = v[y * 96 : (y + 1) * 96]
 
 
+def near(u):
+    return u + 1 - 2 * (u % 2)
+
+
+def far(u):
+    return 3 - u
+
+
+def over(u):
+    return (u + 2) % 4
+
+
+class Halves:
+    def __init__(self, push, axis, c, slab, got_first, got_second):
+        self.push, self.slab, self.u = push, slab, c[axis]
+        self.got_first, self.got_second = got_first, got_second
+        self.to = lambda place: peer(axis, place + 4 - c[axis])
+        self.one, self.two = {}, []
+
+    def ready(self, which):
+        u = self.u
+        if which == "over":
+            self.one[0, 0] = self.push(self.slab(over(u), 0), self.got_first(0, 0), self.to(near(u)))
+            self.one[1, 0] = self.push(self.slab(over(u), 1), self.got_first(1, 0), self.to(far(u)))
+        elif which == "near":
+            self.one[0, 1] = self.push(self.slab(near(u), 0), self.got_first(0, 1), self.to(near(u)))
+        elif which == "far":
+            self.one[1, 1] = self.push(self.slab(far(u), 1), self.got_first(1, 1), self.to(far(u)))
+
+    def first(self):
+        for which in ("over", "near", "far"):
+            self.ready(which)
+
+    def second(self):
+        u = self.u
+        for h, place in ((0, far(u)), (1, near(u))):
+            self.one[h, 0].wait()
+            at = self.slab(place, h)
+            at[...] = (at[...].astype(F32) + self.got_first(h, 0)[...].astype(F32)).astype(BF16)
+            self.two.append(self.push(at, self.got_second(h), self.to(place)))
+
+    def final(self):
+        for h in range(2):
+            self.one[h, 1].wait()
+            self.two[h].wait()
+            at = self.slab(self.u, h)
+            at[...] = (
+                at[...].astype(F32) + self.got_first(h, 1)[...].astype(F32) + self.got_second(h)[...].astype(F32)
+            ).astype(BF16)
+
+
 def sum_first(buf, got, copies, own):
     for copy in copies:
         copy.wait()
@@ -436,9 +487,9 @@
         xs, gs, (dkv,), (t_ref,) = take(3), take(3), take(1), take(1)
         held = (t_ref, gt_ref)
         acc2, o_acc2, (dq_ref, own_ref) = take(3), take(3), take(2)
-        sendbuf, r1a, r1b, r2, got2 = take(3), take(3), take(3), take(3), take(3)
-        o_buf, o_got1, o_got2 = take(1), take(3), take(3)
-        kv1, kv2, kv3 = take(6), take(6), take(6)
+        sendbuf, r1, r2, t1, t2 = take(3), take(3), take(3), take(3), take(3)
+        o_buf, o_r1, o_r2, o_got2 = take(1), take(3), take(3), take(3)
+        kv1, kv1b, kv2, kv3 = take(6), take(6), take(6), take(6)
         m_got, o_got = take(3), take(3)
         n_parts = len(QKV_PARTS)
         q_got2, q_acc2, q_got3 = (take(n_parts) for _ in range(3))
@@ -446,7 +497,10 @@
         room = ((0, 0, 256), (0, 256, 512), (1, 0, 256), (1, 256, 384), (1, 384, 512))
         q_buf = [xs[m].at[:, :, lo:hi] for m, lo, hi in room]
         room = ((0, 0, 256), (1, 0, 256), (2, 0, 256), (0, 768, 128), (1, 768, 128))
-        q_got1 = [[gs[m].at[0:384, lo + k * n : lo + (k + 1) * n] for k in range(3)] for m, lo, n in room]
+        q_got1 = [
+            [gs[m].at[192 * (k % 2) : 192 * (k % 2) + 192, lo + k // 2 * n : lo + (k // 2 + 1) * n] for k in range(6)]
+            for m, lo, n in room[:3]
+        ] + [[gs[m].at[0:384, lo + k * n : lo + (k + 1) * n] for k in range(3)] for m, lo, n in room[3:]]
         s_acc, s_got, gp_ref, part, got_part = take(5)
         loc, send, recv = take(3)
         c = coords()
@@ -464,65 +518,24 @@
             copy.start()
             return copy
 
-        near = lambda u: u + 1 - 2 * (u % 2)
-        far = lambda u: 3 - u
-        over = lambda u: (u + 2) % 4
-        top, low = pl.ds(0, 192), pl.ds(192, 192)
-        first, second = [[], [], []], [[], [], []]
-
-        def neighbour(axis, u):
-            return peer(axis, u + 4 - c[axis])
-
-        def slab(m, u):
-            return sendbuf[m].at[u]
-
-        def ready(m, which):
-            axis = MLP_AXES[m][1]
-            u = c[axis]
-            if which == "over":
-                first[m].append(push(slab(m, over(u)).at[top, :], r1a[m].at[0], neighbour(axis, near(u))))
-                first[m].append(push(slab(m, over(u)).at[low, :], r1b[m].at[0], neighbour(axis, far(u))))
-            elif which == "near":
-                first[m].append(push(slab(m, near(u)).at[top, :], r1a[m].at[1], neighbour(axis, near(u))))
-            elif which == "far":
-                first[m].append(push(slab(m, far(u)).at[low, :], r1b[m].at[1], neighbour(axis, far(u))))
-
-        def second_step(m):
-            axis = MLP_AXES[m][1]
-            u = c[axis]
-            first[m][0].wait()
-            at = slab(m, far(u)).at[top, :]
-            at[...] = (at[...].astype(F32) + r1a[m][0].astype(F32)).astype(BF16)
-            second[m].append(push(at, r2[m].at[0], neighbour(axis, far(u))))
-            first[m][1].wait()
-            at = slab(m, near(u)).at[low, :]
-            at[...] = (at[...].astype(F32) + r1b[m][0].astype(F32)).astype(BF16)
-            second[m].append(push(at, r2[m].at[1], neighbour(axis, near(u))))
-
-        second_axis = [[], [], []]
-
-        def second_axis_step(m):
-            axis = MLP_AXES[m][1]
-            own = slab(m, c[axis])
-            for copy in first[m][2:] + second[m]:
-                copy.wait()
-            own[top, :] = (own[top, :].astype(F32) + r1a[m][1].astype(F32) + r2[m][0].astype(F32)).astype(BF16)
-            own[low, :] = (own[low, :].astype(F32) + r1b[m][1].astype(F32) + r2[m][1].astype(F32)).astype(BF16)
-            axis = MLP_AXES[m][2]
-            for k in (1, 2, 3):
-                rows = pl.ds(pl.multiple_of(((c[axis] + k) % 4) * 96, 32), 96)
-                second_axis[m].append(push(own.at[rows, :], got2[m].at[k - 1], peer(axis, k)))
-
-        def second_axis_sum(m):
-            for copy in second_axis[m]:
-                copy.wait()
-            rows = pl.ds(pl.multiple_of(c[MLP_AXES[m][2]] * 96, 32), 96)
-            total = slab(m, c[MLP_AXES[m][1]])[rows, :].astype(F32)
-            for k in range(3):
-                total = total + got2[m][k].astype(F32)
-            acc2[m][...] = total
-
-        for name, place in (("over", over), ("near", near), ("far", far), ("own", lambda u: u)):
+        def mlp_slab(m):
+            return lambda u, h: sendbuf[m].at[u, pl.ds(192 * h, 192), :]
+
+        mlp_one = [
+            Halves(push, MLP_AXES[m][1], c, mlp_slab(m), lambda h, i, m=m: r1[m].at[h, i], lambda h, m=m: r2[m].at[h])
+            for m in range(3)
+        ]
+
+        def mlp_rows(m):
+            own = sendbuf[m].at[c[MLP_AXES[m][1]]]
+            return lambda u, h: own.at[pl.ds(pl.multiple_of(u * 96 + h * 48, 16), 48), :]
+
+        mlp_two = [
+            Halves(push, MLP_AXES[m][2], c, mlp_rows(m), lambda h, i, m=m: t1[m].at[h, i], lambda h, m=m: t2[m].at[h])
+            for m in range(3)
+        ]
+
+        for name, place in (("over", over), ("near", near), ("far", far), ("own", lambda v: v)):
             for i, m in enumerate((0, 2, 1)):
                 if name == "over":
                     loads[2 * i].wait()
@@ -530,19 +543,20 @@
                 u = place(c[MLP_AXES[m][1]])
                 x = xs[m][u]
                 sendbuf[m][u] = mm(x, gs[m][...]).astype(BF16)
-                ready(m, name)
-
-        o_first, o_second = [[], [], []], [[], [], []]
-        def out_first(p):
-            order = OUT_ORDERS[p]
-            slab_products(o_buf[p], bt_ref, a_ref[:, p * 256 : (p + 1) * 256], order)
-            for k in (1, 2, 3):
-                there = (c[order[0]] + k) % 4
-                o_first[p].append(push(o_buf[p].at[there], o_got1[p].at[k - 1], peer(order[0], k)))
+                mlp_one[m].ready(name)
+
+        def buf_slab(buf):
+            return lambda u, h: buf.at[u, pl.ds(192 * h, 192), :]
+
+        out_one = [
+            Halves(push, OUT_ORDERS[p][0], c, buf_slab(o_buf[p]), lambda h, i, p=p: o_r1[p].at[h, i], lambda h, p=p: o_r2[p].at[h])
+            for p in range(3)
+        ]
+        o_second = [[], [], []]
 
         def out_second(p):
             order = OUT_ORDERS[p]
-            sum_first(o_buf[p], [o_got1[p].at[k] for k in range(3)], o_first[p], c[order[0]])
+            out_one[p].final()
             for k in (1, 2, 3):
                 rows = pl.ds(pl.multiple_of(((c[order[1]] + k) % 4) * 96, 32), 96)
                 o_second[p].append(push(o_buf[p].at[c[order[0]], rows, :], o_got2[p].at[k - 1], peer(order[1], k)))
@@ -594,15 +608,37 @@
             return 0
 
         kv_pending = [[] for _ in range(6)]
+        kv_parts = [(r0 + 128 * chunk, rn, order) for chunk in range(2) for r0, rn, order in KV_CHUNK]
+
+        def kv_slab(p):
+            r0, rn, order = kv_parts[p]
+            rest = [a for a in AXES if a != order[0]]
+
+            def slab(u, h):
+                where = {order[0]: u, rest[0]: pl.ds(2 * h, 2), rest[1]: slice(None)}
+                return dkv.at[where["z"], where["x"], where["y"], pl.ds(r0, rn), :]
+
+            return slab
+
+        kv_one = [
+            Halves(push, kv_parts[p][2][0], c, kv_slab(p), lambda h, i, p=p: kv1[p].at[h, i], lambda h, p=p: kv1b[p].at[h])
+            for p in range(6)
+        ]
+
+        def kv_halves(chunk, step):
+            for p in range(chunk * 3, chunk * 3 + 3):
+                getattr(kv_one[p], step)()
 
         def kv_stage(chunk, stage):
-            for i, (r0, rn, order) in enumerate(KV_CHUNK):
-                p, r0 = chunk * 3 + i, r0 + chunk * 128
-                for copy in kv_pending[p]:
-                    copy.wait()
-                kv_pending[p] = []
-                got = (kv1, kv2, kv3)
-                if stage:
+            got = (None, kv2, kv3)
+            for p in range(chunk * 3, chunk * 3 + 3):
+                r0, rn, order = kv_parts[p]
+                if stage == 1:
+                    kv_one[p].final()
+                else:
+                    for copy in kv_pending[p]:
+                        copy.wait()
+                    kv_pending[p] = []
                     mine = kv_index(order[stage:], c, r0, rn)
                     own = dkv[mine].astype(F32)
                     for k in range(3):
@@ -612,9 +648,8 @@
                         continue
                     dkv[mine] = own.astype(BF16)
                 for k in (1, 2, 3):
-                    there = (c[order[stage]] + k) % 4
                     cc = dict(c)
-                    cc[order[stage]] = there
+                    cc[order[stage]] = (c[order[stage]] + k) % 4
                     src = dkv.at[kv_index(order[stage + 1 :], cc, r0, rn)]
                     kv_pending[p].append(push(src, got[stage][p].at[k - 1], peer(order[stage], k)))
 
@@ -626,17 +661,27 @@
             return copies
 
         q_copies = [[] for _ in QKV_PARTS]
+        q_one = [
+            Halves(push, QKV_PARTS[p][2][0], c, buf_slab(q_buf[p]), lambda h, i, p=p: q_got1[p][2 * h + i], lambda h, p=p: q_got1[p][4 + h])
+            for p in range(3)
+        ]
 
         def qkv_first(p):
             lo, hi, order = QKV_PARTS[p]
             slab_products(q_buf[p], nt_ref, gp_ref[:, lo:hi], order)
+            if p < 3:
+                q_one[p].first()
+                return
             for k in (1, 2, 3):
                 there = (c[order[0]] + k) % 4
                 q_copies[p].append(push(q_buf[p].at[there], q_got1[p][k - 1], peer(order[0], k)))
 
         def qkv_second(p):
             order = QKV_PARTS[p][2]
-            sum_first(q_buf[p], q_got1[p], q_copies[p], c[order[0]])
+            if p < 3:
+                q_one[p].final()
+            else:
+                sum_first(q_buf[p], q_got1[p], q_copies[p], c[order[0]])
             q_copies[p] = []
             for k in (1, 2, 3):
                 rows = pl.ds(pl.multiple_of(((c[order[1]] + k) % 4) * 96, 32), 96)
@@ -669,23 +714,34 @@
                 else:
                     gv_ref[...] = v
 
+        m_copies = [None] * 3
+
+        def mlp_third(m):
+            mlp_two[m].final()
+            rows = pl.ds(pl.multiple_of(c[MLP_AXES[m][2]] * 96, 32), 96)
+            acc2[m][...] = sendbuf[m][c[MLP_AXES[m][1]], rows, :].astype(F32)
+            m_copies[m] = share(acc2[m], m_got[m], MLP_AXES[m][0])
+
         lax.fori_loop(4, 8, k_step, 0)
-        kv_stage(1, 0)
-        second_step(0)
+        kv_halves(1, "first")
+        mlp_one[0].second()
         lax.fori_loop(0, 1, k_step, 0)
-        second_step(2)
-        second_step(1)
+        mlp_one[2].second()
+        mlp_one[1].second()
+        kv_halves(1, "second")
         lax.fori_loop(1, 2, k_step, 0)
+        for p, order in enumerate(OUT_ORDERS):
+            slab_products(o_buf[p], bt_ref, a_ref[:, p * 256 : (p + 1) * 256], order)
+            out_one[p].first()
+        mlp_one[0].final()
+        mlp_two[0].first()
+        lax.fori_loop(2, 3, k_step, 0)
         kv_stage(1, 1)
-        second_axis_step(0)
-        for p in range(3):
-            out_first(p)
-        lax.fori_loop(2, 3, k_step, 0)
-        kv_stage(1, 2)
-        second_axis_step(2)
-        second_axis_step(1)
+        for m in (2, 1):
+            mlp_one[m].final()
+            mlp_two[m].first()
         lax.fori_loop(3, 4, k_step, 0)
-        kv_stage(0, 0)
+        kv_halves(0, "first")
 
         cos_t, sin_t = cos_ref[...], sin_ref[...]
         for qb in range(8):
@@ -695,13 +751,18 @@
             for h in range(6):
                 v = dq[h * Q_BLK : (h + 1) * Q_BLK]
                 gp_ref[rows, h * 128 : (h + 1) * 128] = (v * cs - swap_halves(v) * sn).astype(BF16)
+        mlp_two[0].second()
+        kv_halves(0, "second")
+        for p in range(3):
+            out_one[p].second()
+        for m in (2, 1):
+            mlp_two[m].second()
         for p in range(3):
             qkv_first(p)
+        kv_stage(1, 2)
         kv_stage(0, 1)
-        m_copies = [None] * 3
         for m in (0, 2, 1):
-            second_axis_sum(m)
-            m_copies[m] = share(acc2[m], m_got[m], MLP_AXES[m][0])
+            mlp_third(m)
         w_ref = [sendbuf[0].at[:, :, h * 128 : (h + 1) * 128] for h in range(8)]
         w_from = [w_hbm[0].at[h] for h in range(6)] + [w_hbm[1], w_hbm[2]]
         w_loads = [pltpu.make_async_copy(w_from[h], w_ref[h], loc.at[7 + n_late + h]) for h in range(8)]
@@ -714,9 +775,11 @@
                 total = total + nt(gp_ref[:, h * 128 : (h + 1) * 128], w_ref[h][...].reshape(1536, 128))
             return total
 
+        kv_stage(0, 2)
         for p in range(3):
             out_second(p)
-        kv_stage(0, 2)
+        for p in range(3):
+            q_one[p].second()
         for copy in loads[7:] + w_loads:
             copy.wait()
         part[...] = back_through(0, 6)
@@ -823,14 +886,16 @@
         + [pltpu.VMEM((96, 256), F32)] * 3
         + [pltpu.VMEM((8, 128, 96), F32), pltpu.VMEM((256, 128), F32)]
         + [pltpu.VMEM((4, 384, FC), BF16)] * 3
+        + [pltpu.VMEM((2, 2, 192, FC), BF16)] * 3
         + [pltpu.VMEM((2, 192, FC), BF16)] * 3
-        + [pltpu.VMEM((2, 192, FC), BF16)] * 3
-        + [pltpu.VMEM((2, 192, FC), BF16)] * 3
-        + [pltpu.VMEM((3, 96, FC), BF16)] * 3
+        + [pltpu.VMEM((2, 2, 48, FC), BF16)] * 3
+        + [pltpu.VMEM((2, 48, FC), BF16)] * 3
         + [pltpu.VMEM((4, 384, 256), BF16)]
-        + [pltpu.VMEM((3, 384, 256), BF16)] * 3
+        + [pltpu.VMEM((2, 2, 192, 256), BF16)] * 3
+        + [pltpu.VMEM((2, 192, 256), BF16)] * 3
         + [pltpu.VMEM((3, 96, 256), BF16)] * 3
-        + [pltpu.VMEM((3, 4, 4, r, 128), BF16) for r in rows]
+        + [pltpu.VMEM((2, 2, 2, 4, r, 128), BF16) for r in rows]
+        + [pltpu.VMEM((2, 2, 4, r, 128), BF16) for r in rows]
         + [pltpu.VMEM((3, 4, r, 128), BF16) for r in rows]
         + [pltpu.VMEM((3, r, 128), BF16) for r in rows]
         + [pltpu.VMEM((3, 24, FC), F32)] * 3
@@ -845,8 +910,8 @@
             pltpu.VMEM((128, 1536), F32),
             pltpu.VMEM((128, 1536), F32),
             DMA((7 + n_late + 8,)),
-            DMA((192,)),
-            DMA((192,)),
+            DMA((224,)),
+            DMA((224,)),
         ]
     )
     vm, sm, hbm = (pl.BlockSpec(memory_space=m) for m in (pltpu.VMEM, pltpu.SMEM, pl.ANY))

time: 216 us -> 205 us (0.949)
  Pallas kernels: 206 us -> 195 us
    pallas_call x1, Pallas kernels: 118 us -> 106 us  [backward(): pl.pallas_call(body, out_shape=shape, in_specs=[sm] + [hbm] * (10 + n_lat...]
where the time goes in v3:
time: 205 us; the launch traced here: 201 us
  Pallas kernels  195 us (95%)
  local copies, waits for them, and re-layouts  4.69 us (2%)
    pallas_call x1, Pallas kernels, backward(): pl.pallas_call(body, out_shape=shape, in_specs=[sm] + [hbm] * (10 + n_lat...  106 us
    pallas_call x1, Pallas kernels, forward(): pl.pallas_call(body, out_shape=(f32(128, 1536), f32(128, 1536), b16(1536,...  85.4 us

profile of v3, /device:TPU:0, one launch (start us, length us, event | category | flops | bytes accessed | tf_op | source)
XLA Modules:
  0.0 201.0 jit_solution(8175638496915615617)
XLA Ops:
  0.6 0.7 stack.10
  1.3 0.7 stack.9
  2.0 0.6 pad_maximum_fusion.g_ref.refs_22_
  2.7 85.4 %forward.1 = (f32[128,1536]{1,0:T(8,128)}, f32[128,1536]{1,0:T(8,128)}, bf16[1536,128]{1,0:T(8,128)(2,1)}, bf16[8,96,128]{2,1,0:T(8,128)(2,1)}, f32[8,1,96]{2,1,...) custom-call(s32[8]{0:T(128)} %refs_0_.1, ...), custom_call_target="tpu_custom_call" | custom-call | tf_op jit(solution)/shard_map/forward/pallas_call | solution.py:369
  88.1 106.5 %backward.1 = (f32[128,1536]{1,0:T(8,128)}, f32[6,24,128]{2,1,0:T(8,128)}, f32[24,128]{1,0:T(8,128)}, f32[24,128]{1,0:T(8,128)}, f32[6,24,128]{2,1,0:T(8,128)}, ...) custom-call(s32[8]{0:T(128)} %refs_0_.1, ...), custom_call_target="tpu_custom_call" | custom-call | tf_op jit(solution)/shard_map/backward/pallas_call | solution.py:921
  194.6 2.9 %hand_out.1 = (f32[128,1536]{1,0:T(8,128)}, f32[128,1536]{1,0:T(8,128)}, f32[6,24,128]{2,1,0:T(8,128)}, f32[24,128]{1,0:T(8,128)}, f32[24,128]{1,0:T(8,128)}, /*...) custom-call(f32[128,1536]{1,0:T(8,128)} %get-tuple-element.51.refs_0_, ...), custom_call_target="tpu_custom_call" | custom-call | tf_op jit(solution)/shard_map/hand_out/pallas_call | solution.py:948
  197.5 1.4 fusion
  198.9 0.7 dynamic_slice.10
  199.6 0.7 copy.29
  200.3 0.5 fusion.1
